TPU v7x, 32 devices: a whole 2x2x4 slice. The times are simulated.
32 devices in a mesh: groups: 2 (over x), dp: 8 (over z, y), tensor: 2 (over core).
Axes of the slice: x: 2, y: 2, z: 4, core: 2. Of those that a mesh axis runs over, the one named last changes fastest.
Arguments:
- normed_hidden_states: bfloat16 [4096, 8192], P(('groups', 'dp'), 'tensor'), parts along dimension 0, may hold values from -6 to 6
- value_base_matrix: bfloat16 [8192, 1024], P('tensor'), may hold values from -0.0625 to 0.0625
- down_factor_slots: bfloat16 [512, 64, 8192], P(('groups', 'dp'), None, 'tensor'), parts along dimension 0, may hold values from -0.0625 to 0.0625
- up_factor_slots: bfloat16 [512, 64, 1024], P(('groups', 'dp'), None, 'tensor'), parts along dimension 0, may hold values from -0.75 to 0.75
- row_adapter_index: int32 [4096], P(('groups', 'dp')), parts along dimension 0, may hold values from 0 to 255, as said below
- adapter_slot_table: int32 [512], P('groups'), parts along dimension 0, may hold values from 0 to 255, as said below
Outputs:
- projected: bfloat16 [4096, 1024], P(('groups', 'dp'), 'tensor'), parts along dimension 0
There are 2 independent parts, one for each index of `groups`. A program takes and returns all parts, laid end to end along the dimension named above; an argument that names none is the same for every part. Nothing has to cross between parts.
Inputs may be any that keep to these rules, and one draw needn't show every extreme that they name: `row_adapter_index`: the ids of one device's 256 rows (an aligned block) do not fall. Call slots k * 32 to (k + 1) * 32 - 1 the k-th slot block: at most 128 rows of one aligned block have adapters whose slot lies in one slot block, and in every draw some slot block has exactly 128 rows in every aligned block. `adapter_slot_table`: each slot holds exactly one adapter.
All inputs are finite; a program needn't handle non-finite values.
Results may differ from a plain program's by a relative error of at most 0.005.
Values may be sent and summed in bfloat16 or wider, within the bound.
No kernel may reach another device: no remote copies, remote signals or barrier semaphores. Data moves between devices by JAX's collectives and lax.ppermute only.
A program may use at most 192 MiB of HBM per device.

v0:
```python
import jax
import jax.numpy as jnp
from jax import lax
from jax.sharding import PartitionSpec as P


def on_device(
    normed_hidden_states,
    value_base_matrix,
    down_factor_slots,
    up_factor_slots,
    row_adapter_index,
    adapter_slot_table,
):
    row_count = normed_hidden_states.shape[0]
    peer_count = lax.axis_size("dp")
    resident_adapters = down_factor_slots.shape[0]
    capacity = 4 * row_count // peer_count
    matches = (
        row_adapter_index[:, None]
        == jnp.arange(adapter_slot_table.shape[0], dtype=jnp.int32)[None, :]
    )
    slot_ids = jnp.sum(jnp.where(matches, adapter_slot_table[None, :], 0), axis=1)
    owner_ids = slot_ids // resident_adapters
    local_ids = slot_ids % resident_adapters
    partial_sum = jnp.dot(
        normed_hidden_states, value_base_matrix, preferred_element_type=jnp.float32
    )
    base_sum = lax.psum_scatter(partial_sum, "tensor", scatter_dimension=1, tiled=True)
    owner_hits = (owner_ids[:, None] == jnp.arange(peer_count, dtype=jnp.int32)[None, :]).astype(
        jnp.int32
    )
    position = jnp.sum(jnp.cumsum(owner_hits, axis=0) * owner_hits, axis=1) - 1
    target_ids = owner_ids * capacity + position
    source_ids = (
        jnp.zeros((peer_count * capacity,), jnp.int32)
        .at[target_ids]
        .set(jnp.arange(row_count, dtype=jnp.int32))
    )
    local_slots = (
        jnp.full((peer_count * capacity,), -1.0, jnp.float32)
        .at[target_ids]
        .set(local_ids.astype(jnp.float32))
        .astype(jnp.bfloat16)
    )
    down_use, up_use = (down_factor_slots, up_factor_slots)
    outgoing = normed_hidden_states[source_ids].reshape(peer_count, capacity, -1)
    outgoing_local = local_slots.reshape(peer_count, capacity)
    got_rows = lax.all_to_all(outgoing, "dp", split_axis=0, concat_axis=0, tiled=True)
    got_local = lax.all_to_all(outgoing_local, "dp", split_axis=0, concat_axis=0, tiled=True)
    senders, item_count = got_local.shape
    total_items = senders * item_count
    slot_count = down_use.shape[0]
    rank_size = down_use.shape[1]
    stacked = got_rows.reshape(total_items, got_rows.shape[-1])
    all_ranks = lax.dot_general(
        stacked,
        down_use.reshape(slot_count * rank_size, -1),
        (((1,), (1,)), ((), ())),
        preferred_element_type=jnp.float32,
    )
    all_ranks = all_ranks.reshape(total_items, slot_count, rank_size)
    picked = got_local.reshape(total_items).astype(jnp.float32)
    selector = picked[:, None] == jnp.arange(slot_count, dtype=jnp.float32)[None, :]
    chosen = jnp.sum(jnp.where(selector[:, :, None], all_ranks, jnp.float32(0.0)), axis=1)
    chosen = lax.psum(chosen.reshape(-1), "tensor").reshape(total_items, rank_size)
    rank_projection = chosen.astype(jnp.bfloat16)
    spread = jnp.where(
        selector[:, :, None], rank_projection[:, None, :], jnp.zeros((), jnp.bfloat16)
    )
    spread = spread.reshape(total_items, slot_count * rank_size)
    row_update = jnp.dot(
        spread, up_use.reshape(slot_count * rank_size, -1), preferred_element_type=jnp.float32
    ).astype(jnp.bfloat16)
    returned = lax.all_to_all(
        row_update.reshape(senders, item_count, -1), "dp", split_axis=0, concat_axis=0, tiled=True
    )
    adapter_row_update = returned.reshape(-1, returned.shape[-1])[target_ids]
    return (base_sum + adapter_row_update.astype(jnp.float32)).astype(jnp.bfloat16)


def solution(mesh):
    placed = (
        P(("groups", "dp"), "tensor"),
        P("tensor", None),
        P(("groups", "dp"), None, "tensor"),
        P(("groups", "dp"), None, "tensor"),
        P(("groups", "dp")),
        P("groups"),
    )
    return jax.shard_map(
        on_device,
        mesh=mesh,
        in_specs=placed,
        out_specs=P(("groups", "dp"), "tensor"),
        check_vma=False,
    )
```

profile of v0, /device:TPU:0, one launch (start us, length us, event | category | flops | bytes accessed | tf_op | source)
XLA Modules:
  0.0 288.3 jit_solution(1873308723973259196)
XLA Ops:
  6.5 1.0 select_reduce_fusion.1
  7.6 0.6 reduce-window.6
  8.2 0.2 slice_reduce_fusion
  8.4 0.1 fusion.7
  8.6 1.4 scatter_custom_fusion
  10.0 0.6 copy.11
  10.6 7.3 %all-to-all-start = ((bf16[8,1,128]{2,1,0:T(2,128)(2,1)}), bf16[8,1,128]{2,1,0:T(2,128)(2,1)S(1)}, u32[]{:S(2)}, u32[]{:S(2)}) async-start(bf16[8,1,128]{2,1,0:T(2,128)(2,1)} %copy.11), calls=%async_computation.1 | async-start | bytes 8192 | tf_op jit(solution)/shard_map/all_to_all | solution.py:50
  17.9 1.4 scatter_custom_fusion.1
  19.3 7.8 %gather_fusion = bf16[1024,4096]{1,0:T(8,128)(2,1)} fusion(bf16[256,4096]{1,0:T(8,128)(2,1)S(1)} %copy-done, s32[1024]{0:T(1024)S(1)} %fusion.9), kind=kCustom, calls=%fused_computation | custom fusion | bytes 16781312 | tf_op jit(solution)/shard_map/gather | solution.py:47
  27.1 6.0 %all-to-all-start.1 = ((bf16[8,128,4096]{2,1,0:T(8,128)(2,1)}), bf16[8,128,4096]{2,1,0:T(8,128)(2,1)}, u32[]{:S(2)}, u32[]{:S(2)}) async-start(bf16[8,128,4096]{2,1,0:T(8,128)(2,1)} %bitcast.33), calls=%async_computation.2 | async-start | bytes 16777216 | tf_op jit(solution)/shard_map/all_to_all | solution.py:49
  33.1 0.0 reduce-scatter.2.cloned.1.call-start
  33.2 6.7 %fusion.16 = f32[256,1024]{1,0:T(8,128)} fusion(bf16[256,4096]{1,0:T(8,128)(2,1)S(1)} %copy-done, bf16[4096,1024]{1,0:T(8,128)(2,1)} %param.7), kind=kOutput, calls=%fused_computation.49 | convolution fusion | flops 2147483648 | bytes 11534336 | tf_op jit(solution)/shard_map/dot_general | solution.py:26
  40.0 175.8 %all-to-all-done.1 = bf16[8,128,4096]{2,1,0:T(8,128)(2,1)} async-done(((bf16[8,128,4096]{2,1,0:T(8,128)(2,1)}), bf16[8,128,4096]{2,1,0:T(8,128)(2,1)}, u32[]{:S(2)}, u32[]{:S(2)}) %all-to-all-start.1) | async-done | bytes 8388640 | tf_op jit(solution)/shard_map/all_to_all | solution.py:49
  215.7 22.9 %select_reduce_fusion = f32[1024,64]{0,1:T(8,128)S(1)} fusion(pred[1024,32]{0,1:T(8,128)(4,1)S(1)} %iota_compare_fusion.1, bf16[1024,4096,1]{1,0,2:T(8,128)(2,1)} %bitcast.10, bf16[32,64,4096]{2,1,0:T(8,128)(2,1)} %param.8), kind=kOutput, calls=%fused_computation.4 | convolution fusion | flops 17183997952 | bytes 25460736 | tf_op jit(solution)/shard_map/dot_general | solution.py:56
  238.6 0.2 copy.12
  238.8 0.1 reshape.158
  239.0 4.2 %all-reduce.1 = bf16[65536]{0:T(1024)(128)(2,1)S(1)} all-reduce(f32[65536]{0:T(1024)S(1)} %reshape.158), channel_id=1, replica_groups=mesh['groups'=2,'dp'=8,'tensor'=2] {'tensor'}, use_global_device_ids=true, to_apply=%region_8.9 | all-reduce | flops 65536 | bytes 393216 | tf_op jit(solution)/shard_map/psum | solution.py:66
  243.1 0.1 convert_element_type.46
  243.3 0.1 copy.13
  243.4 5.0 %bitcast_convert_fusion = bf16[1024,512]{1,0:T(8,128)(2,1)} fusion(bf16[32,64,512]{2,1,0:T(8,128)(2,1)} %param.9, pred[1024,32]{0,1:T(8,128)(4,1)S(1)} %iota_compare_fusion.1, bf16[1024,64]{0,1:T(8,128)(2,1)S(1)} %copy.13), kind=kOutput, calls=%fused_computation.8 | convolution fusion | flops 2150105088 | bytes 3309568 | tf_op jit(solution)/shard_map/dot_general | solution.py:72
  248.4 3.6 %all-to-all-start.2 = ((bf16[8,128,512]{2,1,0:T(8,128)(2,1)}), bf16[8,128,512]{2,1,0:T(8,128)(2,1)S(1)}, u32[]{:S(2)}, u32[]{:S(2)}) async-start(bf16[8,128,512]{2,1,0:T(8,128)(2,1)} %bitcast.35), calls=%async_computation.3 | async-start | bytes 2097152 | tf_op jit(solution)/shard_map/all_to_all | solution.py:75
  252.0 26.4 %all-to-all-done.2 = bf16[8,128,512]{2,1,0:T(8,128)(2,1)S(1)} async-done(((bf16[8,128,512]{2,1,0:T(8,128)(2,1)}), bf16[8,128,512]{2,1,0:T(8,128)(2,1)S(1)}, u32[]{:S(2)}, u32[]{:S(2)}) %all-to-all-start.2) | async-done | bytes 1048608 | tf_op jit(solution)/shard_map/all_to_all | solution.py:75
  278.4 1.2 gather_fusion.1
  279.6 1.8 add_convert_fusion
  (18 shorter events, 0.2 us)
Async XLA Ops:
  6.5 12.8 %copy-start = (bf16[256,4096]{1,0:T(8,128)(2,1)S(1)}, bf16[256,4096]{1,0:T(8,128)(2,1)}, u32[]{:S(2)}) copy-start(bf16[256,4096]{1,0:T(8,128)(2,1)} %param.6) | copy-start | bytes 6291460
  10.6 16.6 %all-to-all-start = ((bf16[8,1,128]{2,1,0:T(2,128)(2,1)}), bf16[8,1,128]{2,1,0:T(2,128)(2,1)S(1)}, u32[]{:S(2)}, u32[]{:S(2)}) async-start(bf16[8,1,128]{2,1,0:T(2,128)(2,1)} %copy.11), calls=%async_computation.1 | async-start | bytes 8192 | tf_op jit(solution)/shard_map/all_to_all | solution.py:50
  27.1 188.6 %all-to-all-start.1 = ((bf16[8,128,4096]{2,1,0:T(8,128)(2,1)}), bf16[8,128,4096]{2,1,0:T(8,128)(2,1)}, u32[]{:S(2)}, u32[]{:S(2)}) async-start(bf16[8,128,4096]{2,1,0:T(8,128)(2,1)} %bitcast.33), calls=%async_computation.2 | async-start | bytes 16777216 | tf_op jit(solution)/shard_map/all_to_all | solution.py:49
  33.1 246.5 %reduce-scatter.2.cloned.1.call-start = ((), (), s32[]{:S(2)}) async-start(), calls=%async_computation.4 | async-start | bytes 1572864 | tf_op jit(solution)/shard_map/reduce_scatter | solution.py:29
  248.4 30.1 %all-to-all-start.2 = ((bf16[8,128,512]{2,1,0:T(8,128)(2,1)}), bf16[8,128,512]{2,1,0:T(8,128)(2,1)S(1)}, u32[]{:S(2)}, u32[]{:S(2)}) async-start(bf16[8,128,512]{2,1,0:T(8,128)(2,1)} %bitcast.35), calls=%async_computation.3 | async-start | bytes 2097152 | tf_op jit(solution)/shard_map/all_to_all | solution.py:75
Sparse Core Ops, SparseCore 0:
  40.0 9.8 reduce-scatter.1
where the time goes:
time: 289 us; the launch traced here: 288 us
  waiting for transfers between devices  202 us (70%)
  matrix products  34.5 us (12%)
  starting transfers between devices  17 us (6%)
  between operations  13.5 us (5%)
  local copies, waits for them, and re-layouts  13.2 us (5%)
  blocking collectives  4.17 us (1%)
  other arithmetic  3.65 us (1%)
    all_to_all x1, waiting for transfers between devices, on_device(): lax.all_to_all(outgoing, 'dp', split_axis=0, concat_axis=0, tiled=True)  176 us
    all_to_all x1, waiting for transfers between devices, on_device(): lax.all_to_all(row_update.reshape(senders, item_count, -1), 'dp', split_a...  26.4 us
    dot_general x1, matrix products, on_device(): lax.dot_general(stacked, down_use.reshape(slot_count * rank_size, -1), ((...  22.9 us
    gather x1, local copies, waits for them, and re-layouts, on_device(): normed_hidden_states[source_ids].reshape(peer_count, capacity, -1)  7.82 us
    all_to_all x1, starting transfers between devices, on_device(): lax.all_to_all(outgoing_local, 'dp', split_axis=0, concat_axis=0, tiled=T...  7.28 us
    dot_general x1, matrix products, on_device(): jnp.dot(normed_hidden_states, value_base_matrix, preferred_element_type=j...  6.7 us
    all_to_all x1, starting transfers between devices, on_device(): lax.all_to_all(outgoing, 'dp', split_axis=0, concat_axis=0, tiled=True)  5.99 us
  transfers between devices with their start and end apart: 4, of which 2 were waited for; matrix products, arithmetic and copies ran while one was open for 16% of the time, Pallas kernels for 0%

commit v1 on v0

v1 whole, which is shorter than its diff:
```python
import functools

import jax
import jax.numpy as jnp
from jax import lax
from jax.experimental import pallas as pl
from jax.experimental.pallas import tpu as pltpu
from jax.sharding import PartitionSpec as P

SLOTS_A_STEP = 8
VMEM_BYTES = 48 * 1024 * 1024
LAST = (((1,), (1,)), ((), ()))
FIRST = (((0,), (0,)), ((), ()))


def ranks_kernel(layout, rank, *refs):
    pieces = refs[: len(layout)]
    slot_ref, factors_ref, out_ref, rows_ref = refs[len(layout) :]
    step = pl.program_id(0)
    slots = factors_ref.shape[0] // rank

    @pl.when(step == 0)
    def _():
        out_ref[...] = jnp.zeros_like(out_ref)
        for (row, column), piece in zip(layout, pieces):
            height, width = piece.shape
            rows_ref[row : row + height, column : column + width] = piece[...]

    products = lax.dot_general(
        factors_ref[...], rows_ref[...], LAST, preferred_element_type=jnp.float32
    )
    slot_of_row = slot_ref[...]
    kept = out_ref[...]
    for slot in range(slots):
        kept = jnp.where(
            slot_of_row == step * slots + slot, products[slot * rank : (slot + 1) * rank], kept
        )
    out_ref[...] = kept


def picked_ranks(pieces, slots, factors, rank, column_block=0):
    total_rows = slots.shape[0]
    width = max(column + piece.shape[1] for _, column, piece in pieces)
    height = SLOTS_A_STEP * rank
    whole = lambda step: (0, 0)
    return pl.pallas_call(
        functools.partial(ranks_kernel, [(row, column) for row, column, _ in pieces], rank),
        grid=(factors.shape[0] // height,),
        out_shape=jax.ShapeDtypeStruct((rank, total_rows), jnp.float32),
        in_specs=[pl.BlockSpec(piece.shape, whole) for _, _, piece in pieces]
        + [
            pl.BlockSpec((1, total_rows), whole),
            pl.BlockSpec((height, width), lambda step: (step, column_block)),
        ],
        out_specs=pl.BlockSpec((rank, total_rows), whole),
        scratch_shapes=[pltpu.VMEM((total_rows, width), jnp.bfloat16)],
        compiler_params=pltpu.CompilerParams(vmem_limit_bytes=VMEM_BYTES),
        cost_estimate=pl.CostEstimate(
            flops=2 * total_rows * factors.shape[0] * width,
            bytes_accessed=2 * (total_rows + factors.shape[0]) * width,
            transcendentals=0,
        ),
    )(*[piece for _, _, piece in pieces], slots[None, :], factors)


def updates_kernel(own_ref, peer_ref, slot_ref, factors_ref, out_ref):
    rank = own_ref.shape[0]
    low = (own_ref[...] + peer_ref[...]).astype(jnp.bfloat16).astype(jnp.float32)
    slot_of_row = slot_ref[...]
    spread = jnp.concatenate(
        [
            jnp.where(slot_of_row == slot, low, 0.0).astype(jnp.bfloat16)
            for slot in range(factors_ref.shape[0] // rank)
        ],
        axis=0,
    )
    out_ref[...] = lax.dot_general(
        spread, factors_ref[...], FIRST, preferred_element_type=jnp.float32
    ).astype(out_ref.dtype)


def row_updates(partial_low, slots, factors):
    other = lax.ppermute(partial_low, "tensor", [(0, 1), (1, 0)])
    rows, columns = slots.shape[0], factors.shape[1]
    return pl.pallas_call(
        updates_kernel,
        out_shape=jax.ShapeDtypeStruct((rows, columns), jnp.bfloat16),
        in_specs=[pl.BlockSpec(memory_space=pltpu.VMEM)] * 4,
        out_specs=pl.BlockSpec(memory_space=pltpu.VMEM),
        compiler_params=pltpu.CompilerParams(vmem_limit_bytes=VMEM_BYTES),
        cost_estimate=pl.CostEstimate(
            flops=2 * rows * factors.shape[0] * columns,
            bytes_accessed=2 * factors.shape[0] * columns,
            transcendentals=0,
        ),
    )(partial_low, other, slots[None, :], factors)


def looked_up(ids, table):
    hits = ids[..., None] == jnp.arange(table.shape[0], dtype=jnp.int32)
    return jnp.sum(jnp.where(hits, table, 0), axis=-1)


def after(value, *others):
    return lax.optimization_barrier((value, *others))[0]


def line_relay(hidden, down, up, own_ids, table, rank):
    row_count, width = hidden.shape
    resident = down.shape[0] // rank
    capacity = 4 * row_count // lax.axis_size("dp")
    half = width // 2
    me = lax.axis_index("dp")
    devices = range(8)

    def exchange(value, flip):
        return lax.ppermute(value, "dp", [(i, i ^ flip) for i in devices])

    def middle(value):
        return lax.ppermute(value, "dp", [(i, i ^ 6) for i in devices if i // 2 in (1, 2)])

    def outward(value, flip=0):
        return lax.ppermute(value, "dp", [(i, i ^ 2 ^ flip) for i in devices if i // 2 in (1, 2)])

    ids = lax.all_to_all(jnp.broadcast_to(own_ids, (8, 1, row_count)), "dp", 0, 0, tiled=True)
    ids = ids.reshape(2, 2, 2, row_count)
    for axis, bit in enumerate((4, 2, 1)):
        ids = jnp.where(me & bit != 0, jnp.flip(ids, axis), ids)
    slots = looked_up(ids.reshape(8, row_count), table)

    hidden = after(hidden, ids)
    one, mid = exchange(hidden, 2), middle(hidden)

    pairs = [(0, owner) for owner in devices]
    pairs += [(1, 0), (2, 0), (2, 1), (3, 0), (4, 0), (4, 1), (4, 2), (4, 3), (5, 0), (6, 0), (6, 1), (7, 0)]
    owners = slots // resident
    sources = jnp.stack([owners[source] for source, _ in pairs])
    wanted = jnp.stack([me ^ owner for _, owner in pairs])[:, None]
    hit = sources == wanted
    places = jnp.where(hit, jnp.cumsum(hit.astype(jnp.int32), axis=1) - 1, -1)
    place = {pair: places[n] for n, pair in enumerate(pairs)}
    order = jnp.arange(capacity, dtype=jnp.int32)[:, None]

    def one_hot(place):
        return (order == place[None, :]).astype(jnp.bfloat16)

    def compact(place, piece):
        return jnp.dot(one_hot(place), piece, preferred_element_type=jnp.float32).astype(
            jnp.bfloat16
        )

    def split_rows(source, rows):
        pair = exchange(compact(place[source, 1], rows), 1)
        return [(0, 0, compact(place[source, 0], rows)), (capacity, 0, pair)]

    def compact_slots(*sources):
        local = slots % resident
        lists = [
            jnp.sum(jnp.where(order == place[f, 0][None, :], local[f][None, :] + 1, 0), axis=1) - 1
            for f in sources
        ]
        return jnp.concatenate(lists)

    back = {}
    slots_0, slots_1 = compact_slots(0, 1), compact_slots(2, 3)
    slots_2, slots_3 = compact_slots(4, 5), compact_slots(6, 7)

    rows_0 = split_rows(0, hidden)
    update_0 = row_updates(picked_ranks(rows_0, slots_0, down, rank), slots_0, up)
    back[0], back[1] = update_0[:capacity], exchange(update_0[capacity:], 1)

    edge = (me // 2 == 0) | (me // 2 == 3)
    two = jnp.where(edge, outward(mid), middle(one))

    rows_1 = split_rows(2, one)
    low_1 = picked_ranks(rows_1, after(slots_1, update_0), down, rank)
    update_1 = row_updates(low_1, slots_1, up)
    back[2], back[3] = exchange(update_1[:capacity], 2), exchange(update_1[capacity:], 3)

    rows_mid = split_rows(6, mid)
    low_mid = picked_ranks(rows_mid, after(slots_3, update_1), down, rank)

    def last_hop(rows):
        straight, across = outward(compact(place[4, 2], rows)), outward(compact(place[4, 3], rows), 1)
        return [(0, 0, straight), (capacity, 0, across)]

    rows_3a, rows_3b = last_hop(two[:, :half]), last_hop(two[:, half:])

    rows_2 = split_rows(4, two)
    low_a = picked_ranks(rows_3a, after(slots_3, low_mid), down, rank, 0)
    low_2 = picked_ranks(rows_2, after(slots_2, low_a), down, rank)
    update_2 = row_updates(low_2, slots_2, up)
    back[4], back[5] = exchange(update_2[:capacity], 4), exchange(update_2[capacity:], 5)

    low_b = picked_ranks(rows_3b, after(slots_3, update_2), down, rank, 1)
    update_3 = row_updates(low_mid + low_a + low_b, slots_3, up)
    back[6], back[7] = exchange(update_3[:capacity], 6), exchange(update_3[capacity:], 7)

    def spread_back(owners):
        return lax.dot_general(
            jnp.concatenate([one_hot(place[0, owner]) for owner in owners]),
            jnp.concatenate([back[owner] for owner in owners]),
            FIRST,
            preferred_element_type=jnp.float32,
        )

    return spread_back(range(6)) + spread_back((6, 7))


def all_to_all_relay(hidden, down, up, own_ids, table, rank):
    row_count = hidden.shape[0]
    peers = lax.axis_size("dp")
    resident = down.shape[0] // rank
    capacity = 4 * row_count // peers
    own_slots = looked_up(own_ids, table)
    hits = (own_slots // resident)[:, None] == jnp.arange(peers, dtype=jnp.int32)[None, :]
    place = jnp.sum(jnp.cumsum(hits.astype(jnp.int32), axis=0) * hits, axis=1) - 1
    target = (own_slots // resident) * capacity + place
    picks = jnp.arange(peers * capacity, dtype=jnp.int32)[:, None] == target[None, :]
    outgoing = jnp.dot(
        picks.astype(jnp.bfloat16), hidden, preferred_element_type=jnp.float32
    ).astype(jnp.bfloat16)
    outgoing_slots = jnp.sum(
        jnp.where(picks, (own_slots % resident)[None, :].astype(jnp.float32) + 1.0, 0.0), axis=1
    ) - 1.0

    def swap(value):
        return lax.all_to_all(
            value.reshape((peers, capacity) + value.shape[1:]), "dp", 0, 0, tiled=True
        ).reshape((peers * capacity,) + value.shape[1:])

    rows = swap(outgoing)
    slots = swap(outgoing_slots).astype(jnp.int32)
    ranks = lax.dot_general(rows, down, LAST, preferred_element_type=jnp.float32)
    selector = slots[:, None] == jnp.arange(resident, dtype=jnp.int32)[None, :]
    low = jnp.sum(
        jnp.where(selector[:, :, None], ranks.reshape(-1, resident, rank), 0.0), axis=1
    )
    low = (low + lax.ppermute(low, "tensor", [(0, 1), (1, 0)])).astype(jnp.bfloat16)
    spread = jnp.where(selector[:, :, None], low[:, None, :], jnp.zeros((), jnp.bfloat16))
    update = jnp.dot(
        spread.reshape(-1, resident * rank), up, preferred_element_type=jnp.float32
    ).astype(jnp.bfloat16)
    return swap(update)[target].astype(jnp.float32)


def on_device(
    normed_hidden_states,
    value_base_matrix,
    down_factor_slots,
    up_factor_slots,
    row_adapter_index,
    adapter_slot_table,
):
    resident, rank, width = down_factor_slots.shape
    partial_sum = jnp.dot(
        normed_hidden_states, value_base_matrix, preferred_element_type=jnp.float32
    )
    base_sum = lax.psum_scatter(partial_sum, "tensor", scatter_dimension=1, tiled=True)
    relay = line_relay if lax.axis_size("dp") == 8 else all_to_all_relay
    adapter_update = relay(
        normed_hidden_states,
        down_factor_slots.reshape(resident * rank, width),
        up_factor_slots.reshape(resident * rank, -1),
        row_adapter_index,
        adapter_slot_table,
        rank,
    )
    return (base_sum + adapter_update).astype(jnp.bfloat16)


def solution(mesh):
    placed = (
        P(("groups", "dp"), "tensor"),
        P("tensor", None),
        P(("groups", "dp"), None, "tensor"),
        P(("groups", "dp"), None, "tensor"),
        P(("groups", "dp")),
        P("groups"),
    )
    return jax.shard_map(
        on_device,
        mesh=mesh,
        in_specs=placed,
        out_specs=P(("groups", "dp"), "tensor"),
        check_vma=False,
    )
```

time: 289 us -> 251 us (0.87)
  waiting for transfers between devices: 202 us -> 127 us
  Pallas kernels: 0 us -> 49 us
  matrix products: 34.5 us -> 14.7 us
  starting transfers between devices: 17 us -> 36.7 us
  local copies, waits for them, and re-layouts: 13.2 us -> 2.39 us
  blocking collectives: 4.17 us -> 0 us
    all_to_all x3 -> x1, waiting for transfers between devices: 202 us -> 0.01 us  [line_relay(): lax.all_to_all(jnp.broadcast_to(own_ids, (8, 1, row_count)), 'dp', 0, 0,...]
    ppermute x0 -> x23, waiting for transfers between devices: none -> 127 us  [the longest x12 104 us: exchange(): return lax.ppermute(value, 'dp', [(i, i ^ flip) for i in devices])]
    pallas_call x0 -> x10, Pallas kernels: none -> 49 us  [the longest x6 46 us: picked_ranks(): pl.pallas_call(functools.partial(ranks_kernel, [(row, column) for row, co...]
    ppermute x0 -> x23, starting transfers between devices: none -> 29.3 us  [the longest x12 19.5 us: exchange(): return lax.ppermute(value, 'dp', [(i, i ^ flip) for i in devices])]
    dot_general x2 -> x14, matrix products: 27.8 us -> 7.25 us  [the longest x12 4.82 us: compact(): jnp.dot(one_hot(place), piece, preferred_element_type=jnp.float32)]
    all_to_all x3 -> x1, starting transfers between devices: 16.9 us -> 7.28 us  [line_relay(): lax.all_to_all(jnp.broadcast_to(own_ids, (8, 1, row_count)), 'dp', 0, 0,...]
    gather x2 -> x0, local copies, waits for them, and re-layouts: 8.98 us -> none  [the longest x1 7.82 us: on_device(): normed_hidden_states[source_ids].reshape(peer_count, capacity, -1)]
    psum x1 -> x0, blocking collectives: 4.17 us -> none  [on_device(): lax.psum(chosen.reshape(-1), 'tensor').reshape(total_items, rank_size)]
  transfers between devices with their start and end apart: 4 -> 25, of which waited for: 2 -> 13; matrix products, arithmetic and copies ran while one was open for 16% -> 7% of each run, Pallas kernels for 0% -> 20%
where the time goes in v1:
time: 251 us; the launch traced here: 247 us
  waiting for transfers between devices  127 us (51%)
  Pallas kernels  49 us (20%)
  starting transfers between devices  36.7 us (15%)
  matrix products  14.7 us (6%)
  between operations  14.1 us (6%)
  other arithmetic  3.09 us (1%)
    ppermute x12, waiting for transfers between devices, exchange(): return lax.ppermute(value, 'dp', [(i, i ^ flip) for i in devices])  104 us
    pallas_call x6, Pallas kernels, picked_ranks(): pl.pallas_call(functools.partial(ranks_kernel, [(row, column) for row, co...  46 us
    ppermute x5, waiting for transfers between devices, outward(): lax.ppermute(value, 'dp', [(i, i ^ 2 ^ flip) for i in devices if i // 2 i...  20.4 us
    ppermute x12, starting transfers between devices, exchange(): return lax.ppermute(value, 'dp', [(i, i ^ flip) for i in devices])  19.5 us
    dot_general x1, matrix products, on_device(): jnp.dot(normed_hidden_states, value_base_matrix, preferred_element_type=j...  7.47 us
    all_to_all x1, starting transfers between devices, line_relay(): lax.all_to_all(jnp.broadcast_to(own_ids, (8, 1, row_count)), 'dp', 0, 0,...  7.28 us
    ppermute x5, starting transfers between devices, outward(): lax.ppermute(value, 'dp', [(i, i ^ 2 ^ flip) for i in devices if i // 2 i...  6.62 us
  transfers between devices with their start and end apart: 25, of which 13 were waited for; matrix products, arithmetic and copies ran while one was open for 7% of the time, Pallas kernels for 20%

profile of v1, /device:TPU:0, one launch (start us, length us, event | category | flops | bytes accessed | tf_op | source)
XLA Modules:
  0.0 247.5 jit_solution(17321852902277331423)
XLA Ops:
  7.8 7.3 %all-to-all-start = ((s32[8,1,256]{2,1,0:T(1,128)}), s32[8,1,256]{2,1,0:T(1,128)S(1)}, u32[]{:S(2)}, u32[]{:S(2)}) async-start(s32[8,1,256]{2,1,0:T(1,128)} %broadcast_in_dim.114), calls=%async_computation.1 | async-start | bytes 16384 | tf_op jit(solution)/shard_map/all_to_all | solution.py:125
  15.2 7.5 %fusion.43 = f32[256,1024]{1,0:T(8,128)} fusion(bf16[256,4096]{1,0:T(8,128)(2,1)} %param.6, bf16[4096,1024]{1,0:T(8,128)(2,1)} %param.7), kind=kOutput, calls=%fused_computation.133 | convolution fusion | flops 2147483648 | bytes 11534336 | tf_op jit(solution)/shard_map/dot_general | solution.py:256
  25.5 2.1 collective-permute-start.3
  32.1 21.1 %collective-permute-done.refs_1_ = bf16[128,4096]{1,0:T(8,128)(2,1)S(1)} collective-permute-done((bf16[128,4096]{1,0:T(8,128)(2,1)S(1)}, bf16[128,4096]{1,0:T(8,128)(2,1)S(1)}, u32[]{:S(2)}, u32[]{:S(2)}) %collective-permute-start) | collective-permute-done | bytes 1048608 | tf_op jit(solution)/shard_map/ppermute | solution.py:117
  53.2 8.8 %shard_map.64.own_ref = f32[64,256]{1,0:T(8,128)S(1)} custom-call(bf16[128,4096]{1,0:T(8,128)(2,1)S(1)} %convolution_convert_fusion.7.refs_0_, bf16[128,4096]{1,0:T(8,128)(2,1)S(1)} %collective-permute-done.refs_1_, s32[1,256]{1,0:T(1,128)S(1)} %bitcast.97, bf16[2048,4096]{1,0:T(8,128)(2,1)} %bitcast.99), custom_call_target="tpu_custom_call" | custom-call | flops 4294967296 | bytes 18874368 | tf_op jit(solution)/shard_map/pallas_call | solution.py:46
  64.1 8.6 %collective-permute-done.3 = bf16[256,4096]{1,0:T(8,128)(2,1)S(1)} collective-permute-done((bf16[256,4096]{1,0:T(8,128)(2,1)S(1)}, bf16[256,4096]{1,0:T(8,128)(2,1)S(1)}, u32[]{:S(2)}, u32[]{:S(2)}) %collective-permute-start.3) | collective-permute-done | bytes 2097184 | tf_op jit(solution)/shard_map/ppermute | solution.py:117
  75.3 24.4 %collective-permute-done.2 = bf16[128,512]{1,0:T(8,128)(2,1)S(1)} collective-permute-done((bf16[128,512]{1,0:T(8,128)(2,1)S(1)}, bf16[128,512]{1,0:T(8,128)(2,1)S(1)}, u32[]{:S(2)}, u32[]{:S(2)}) %collective-permute-start.2) | collective-permute-done | bytes 131104 | tf_op jit(solution)/shard_map/ppermute | solution.py:117
  99.7 2.0 collective-permute-start.10
  105.6 8.6 %shard_map.66.own_ref = f32[64,256]{1,0:T(8,128)S(1)} custom-call(bf16[128,4096]{1,0:T(8,128)(2,1)S(1)} %convolution_convert_fusion.5.refs_0_, bf16[128,4096]{1,0:T(8,128)(2,1)S(1)} %collective-permute-done.4.refs_1_, s32[1,256]{1,0:T(1,128)S(1)} %bitcast.95, bf16[2048,4096]{1,0:T(8,128)(2,1)} %bitcast.100), custom_call_target="tpu_custom_call" | custom-call | flops 4294967296 | bytes 18874368 | tf_op jit(solution)/shard_map/pallas_call | solution.py:46
  116.4 3.0 %collective-permute-start.6 = (bf16[128,512]{1,0:T(8,128)(2,1)S(1)}, bf16[128,512]{1,0:T(8,128)(2,1)S(1)}, u32[]{:S(2)}, u32[]{:S(2)}) collective-permute-start(bf16[128,512]{1,0:T(8,128)(2,1)S(1)} %get-tuple-element.20), channel_id=1, source_target_pairs={{0,4},{2,6},{4,0},{6,2},{8,12},{10,14},{12,8},{14,10},{1,5},{3,7},... | collective-permute-start | bytes 393224 | tf_op jit(solution)/shard_map/ppermute | solution.py:117
  119.5 7.1 %collective-permute-done.14.refs_1_ = bf16[128,4096]{1,0:T(8,128)(2,1)S(1)} collective-permute-done((bf16[128,4096]{1,0:T(8,128)(2,1)S(1)}, bf16[128,4096]{1,0:T(8,128)(2,1)S(1)}, u32[]{:S(2)}, u32[]{:S(2)}) %collective-permute-start.14) | collective-permute-done | bytes 1048608 | tf_op jit(solution)/shard_map/ppermute | solution.py:117
  126.5 8.6 %shard_map.68 = f32[64,256]{1,0:T(8,128)S(1)} custom-call(bf16[128,4096]{1,0:T(8,128)(2,1)S(1)} %convolution_convert_fusion.1.refs_0_, bf16[128,4096]{1,0:T(8,128)(2,1)S(1)} %collective-permute-done.14.refs_1_, s32[1,256]{1,0:T(1,128)S(1)} %bitcast.89, bf16[2048,4096]{1,0:T(8,128)(2,1)} %bitcast.101), custom_call_target="tpu_custom_call" | custom-call | flops 4294967296 | bytes 18874368 | tf_op jit(solution)/shard_map/pallas_call | solution.py:46
  135.2 17.9 %collective-permute-done.6 = bf16[128,512]{1,0:T(8,128)(2,1)S(1)} collective-permute-done((bf16[128,512]{1,0:T(8,128)(2,1)S(1)}, bf16[128,512]{1,0:T(8,128)(2,1)S(1)}, u32[]{:S(2)}, u32[]{:S(2)}) %collective-permute-start.6) | collective-permute-done | bytes 131104 | tf_op jit(solution)/shard_map/ppermute | solution.py:117
  160.8 9.6 %collective-permute-done.12.refs_0_ = bf16[128,2048]{1,0:T(8,128)(2,1)S(1)} collective-permute-done((bf16[128,2048]{1,0:T(8,128)(2,1)S(1)}, bf16[128,2048]{1,0:T(8,128)(2,1)S(1)}, u32[]{:S(2)}, u32[]{:S(2)}) %collective-permute-start.12) | collective-permute-done | bytes 524320 | tf_op jit(solution)/shard_map/ppermute | solution.py:123
  171.7 10.8 %collective-permute-done.13.refs_1_ = bf16[128,2048]{1,0:T(8,128)(2,1)S(1)} collective-permute-done((bf16[128,2048]{1,0:T(8,128)(2,1)S(1)}, bf16[128,2048]{1,0:T(8,128)(2,1)S(1)}, u32[]{:S(2)}, u32[]{:S(2)}) %collective-permute-start.13) | collective-permute-done | bytes 524320 | tf_op jit(solution)/shard_map/ppermute | solution.py:123
  182.5 5.7 %shard_map.69 = f32[64,256]{1,0:T(8,128)S(1)} custom-call(bf16[128,2048]{1,0:T(8,128)(2,1)S(1)} %collective-permute-done.12.refs_0_, bf16[128,2048]{1,0:T(8,128)(2,1)S(1)} %collective-permute-done.13.refs_1_, s32[1,256]{1,0:T(1,128)S(1)} %bitcast.90, bf16[2048,4096]{1,0:T(8,128)(2,1)} %bitcast.102), custom_call_target="tpu_custom_call" | custom-call | flops 2147483648 | bytes 9437184 | tf_op jit(solution)/shard_map/pallas_call | solution.py:46
  188.2 11.4 %collective-permute-done.11.refs_1_ = bf16[128,4096]{1,0:T(8,128)(2,1)S(1)} collective-permute-done((bf16[128,4096]{1,0:T(8,128)(2,1)S(1)}, bf16[128,4096]{1,0:T(8,128)(2,1)S(1)}, u32[]{:S(2)}, u32[]{:S(2)}) %collective-permute-start.11) | collective-permute-done | bytes 1048608 | tf_op jit(solution)/shard_map/ppermute | solution.py:117
  199.7 8.6 %shard_map.70.own_ref = f32[64,256]{1,0:T(8,128)S(1)} custom-call(bf16[128,4096]{1,0:T(8,128)(2,1)S(1)} %convolution_convert_fusion.3.refs_0_, bf16[128,4096]{1,0:T(8,128)(2,1)S(1)} %collective-permute-done.11.refs_1_, s32[1,256]{1,0:T(1,128)S(1)} %bitcast.93, bf16[2048,4096]{1,0:T(8,128)(2,1)} %bitcast.103), custom_call_target="tpu_custom_call" | custom-call | flops 4294967296 | bytes 18874368 | tf_op jit(solution)/shard_map/pallas_call | solution.py:46
  210.4 5.7 %shard_map.72 = f32[64,256]{1,0:T(8,128)S(1)} custom-call(bf16[128,2048]{1,0:T(8,128)(2,1)S(1)} %collective-permute-done.18.refs_0_, bf16[128,2048]{1,0:T(8,128)(2,1)S(1)} %collective-permute-done.19.refs_1_, s32[1,256]{1,0:T(1,128)S(1)} %bitcast.91, bf16[2048,4096]{1,0:T(8,128)(2,1)} %bitcast.104), custom_call_target="tpu_custom_call" | custom-call | flops 2147483648 | bytes 9437184 | tf_op jit(solution)/shard_map/pallas_call | solution.py:46
  216.4 3.5 %collective-permute-start.17 = (bf16[128,512]{1,0:T(8,128)(2,1)S(1)}, bf16[128,512]{1,0:T(8,128)(2,1)S(1)}, u32[]{:S(2)}, u32[]{:S(2)}) collective-permute-start(bf16[128,512]{1,0:T(8,128)(2,1)S(1)} %get-tuple-element.17), channel_id=1, source_target_pairs={{0,10},{2,8},{4,14},{6,12},{8,2},{10,0},{12,6},{14,4},{1,11},{3,9}... | collective-permute-start | bytes 393224 | tf_op jit(solution)/shard_map/ppermute | solution.py:117
  220.7 3.0 %collective-permute-start.21 = (bf16[128,512]{1,0:T(8,128)(2,1)S(1)}, bf16[128,512]{1,0:T(8,128)(2,1)S(1)}, u32[]{:S(2)}, u32[]{:S(2)}) collective-permute-start(bf16[128,512]{1,0:T(8,128)(2,1)S(1)} %get-tuple-element.23), channel_id=1, source_target_pairs={{0,12},{2,14},{4,8},{6,10},{8,4},{10,6},{12,0},{14,2},{1,13},{3,15... | collective-permute-start | bytes 393224 | tf_op jit(solution)/shard_map/ppermute | solution.py:117
  224.9 9.6 %collective-permute-done.16 = bf16[128,512]{1,0:T(8,128)(2,1)S(1)} collective-permute-done((bf16[128,512]{1,0:T(8,128)(2,1)S(1)}, bf16[128,512]{1,0:T(8,128)(2,1)S(1)}, u32[]{:S(2)}, u32[]{:S(2)}) %collective-permute-start.16) | collective-permute-done | bytes 131104 | tf_op jit(solution)/shard_map/ppermute | solution.py:117
  234.6 3.5 %collective-permute-done.17 = bf16[128,512]{1,0:T(8,128)(2,1)S(1)} collective-permute-done((bf16[128,512]{1,0:T(8,128)(2,1)S(1)}, bf16[128,512]{1,0:T(8,128)(2,1)S(1)}, u32[]{:S(2)}, u32[]{:S(2)}) %collective-permute-start.17) | collective-permute-done | bytes 131104 | tf_op jit(solution)/shard_map/ppermute | solution.py:117
  238.5 2.2 fusion.1
  (125 shorter events, 32.5 us)
Async XLA Ops:
  7.8 15.0 %all-to-all-start = ((s32[8,1,256]{2,1,0:T(1,128)}), s32[8,1,256]{2,1,0:T(1,128)S(1)}, u32[]{:S(2)}, u32[]{:S(2)}) async-start(s32[8,1,256]{2,1,0:T(1,128)} %broadcast_in_dim.114), calls=%async_computation.1 | async-start | bytes 16384 | tf_op jit(solution)/shard_map/all_to_all | solution.py:125
  15.1 223.3 %reduce-scatter.2.cloned.1.call-start = ((), (), s32[]{:S(2)}) async-start(), calls=%async_computation.2 | async-start | bytes 1572864 | tf_op jit(solution)/shard_map/reduce_scatter | solution.py:259
  25.5 47.2 %collective-permute-start.3 = (bf16[256,4096]{1,0:T(8,128)(2,1)S(1)}, bf16[256,4096]{1,0:T(8,128)(2,1)S(1)}, u32[]{:S(2)}, u32[]{:S(2)}) collective-permute-start(bf16[256,4096]{1,0:T(8,128)(2,1)S(1)} %copy-done.1), channel_id=1, source_target_pairs={{0,4},{2,6},{4,0},{6,2},{8,12},{10,14},{12,8},{14,10},{1,5},{3,7},... | collective-permute-start | bytes 6291464 | tf_op jit(solution)/shard_map/ppermute | solution.py:117
  27.6 74.2 %collective-permute-start.8 = (bf16[256,4096]{1,0:T(8,128)(2,1)S(1)}, bf16[256,4096]{1,0:T(8,128)(2,1)S(1)}, u32[]{:S(2)}, u32[]{:S(2)}) collective-permute-start(bf16[256,4096]{1,0:T(8,128)(2,1)S(1)} %copy-done.1), channel_id=1, source_target_pairs={{4,8},{6,10},{8,4},{10,6},{5,9},{7,11},{9,5},{11,7},{20,24},{22,26... | collective-permute-start | bytes 6291464 | tf_op jit(solution)/shard_map/ppermute | solution.py:120
  29.1 24.1 %collective-permute-start = (bf16[128,4096]{1,0:T(8,128)(2,1)S(1)}, bf16[128,4096]{1,0:T(8,128)(2,1)S(1)}, u32[]{:S(2)}, u32[]{:S(2)}) collective-permute-start(bf16[128,4096]{1,0:T(8,128)(2,1)S(1)} %convolution_convert_fusion.6), channel_id=1, source_target_pairs={{0,2},{2,0},{4,6},{6,4},{8,10},{10,8},{12,14},{14,12},{1,3},{3,1},... | collective-permute-start | bytes 3145736 | tf_op jit(solution)/shard_map/ppermute | solution.py:117
  62.0 1.3 collective-permute-start.1
  73.1 32.5 %collective-permute-start.4 = (bf16[128,4096]{1,0:T(8,128)(2,1)S(1)}, bf16[128,4096]{1,0:T(8,128)(2,1)S(1)}, u32[]{:S(2)}, u32[]{:S(2)}) collective-permute-start(bf16[128,4096]{1,0:T(8,128)(2,1)S(1)} %convolution_convert_fusion.4), channel_id=1, source_target_pairs={{0,2},{2,0},{4,6},{6,4},{8,10},{10,8},{12,14},{14,12},{1,3},{3,1},... | collective-permute-start | bytes 3145736 | tf_op jit(solution)/shard_map/ppermute | solution.py:117
  74.9 24.8 %collective-permute-start.2 = (bf16[128,512]{1,0:T(8,128)(2,1)S(1)}, bf16[128,512]{1,0:T(8,128)(2,1)S(1)}, u32[]{:S(2)}, u32[]{:S(2)}) collective-permute-start(bf16[128,512]{1,0:T(8,128)(2,1)S(1)} %get-tuple-element.21), channel_id=1, source_target_pairs={{0,2},{2,0},{4,6},{6,4},{8,10},{10,8},{12,14},{14,12},{1,3},{3,1},... | collective-permute-start | bytes 393224 | tf_op jit(solution)/shard_map/ppermute | solution.py:117
  99.7 53.4 %collective-permute-start.10 = (bf16[256,4096]{1,0:T(8,128)(2,1)S(1)}, bf16[256,4096]{1,0:T(8,128)(2,1)}, u32[]{:S(2)}, u32[]{:S(2)}) collective-permute-start(bf16[256,4096]{1,0:T(8,128)(2,1)S(1)} %collective-permute-done.3), channel_id=1, source_target_pairs={{4,8},{6,10},{8,4},{10,6},{5,9},{7,11},{9,5},{11,7},{20,24},{22,26... | collective-permute-start | bytes 6291464 | tf_op jit(solution)/shard_map/ppermute | solution.py:120
  101.7 51.4 %collective-permute-start.9 = (bf16[256,4096]{1,0:T(8,128)(2,1)S(1)}, bf16[256,4096]{1,0:T(8,128)(2,1)S(1)}, u32[]{:S(2)}, u32[]{:S(2)}) collective-permute-start(bf16[256,4096]{1,0:T(8,128)(2,1)S(1)} %collective-permute-done.8), channel_id=1, source_target_pairs={{4,0},{6,2},{8,12},{10,14},{5,1},{7,3},{9,13},{11,15},{20,16},{22,... | collective-permute-start | bytes 6291464 | tf_op jit(solution)/shard_map/ppermute | solution.py:123
  103.7 22.9 %collective-permute-start.14 = (bf16[128,4096]{1,0:T(8,128)(2,1)S(1)}, bf16[128,4096]{1,0:T(8,128)(2,1)S(1)}, u32[]{:S(2)}, u32[]{:S(2)}) collective-permute-start(bf16[128,4096]{1,0:T(8,128)(2,1)S(1)} %convolution_convert_fusion), channel_id=1, source_target_pairs={{0,2},{2,0},{4,6},{6,4},{8,10},{10,8},{12,14},{14,12},{1,3},{3,1},... | collective-permute-start | bytes 3145736 | tf_op jit(solution)/shard_map/ppermute | solution.py:117
  114.3 1.3 collective-permute-start.5
  116.4 36.7 %collective-permute-start.6 = (bf16[128,512]{1,0:T(8,128)(2,1)S(1)}, bf16[128,512]{1,0:T(8,128)(2,1)S(1)}, u32[]{:S(2)}, u32[]{:S(2)}) collective-permute-start(bf16[128,512]{1,0:T(8,128)(2,1)S(1)} %get-tuple-element.20), channel_id=1, source_target_pairs={{0,4},{2,6},{4,0},{6,2},{8,12},{10,14},{12,8},{14,10},{1,5},{3,7},... | collective-permute-start | bytes 393224 | tf_op jit(solution)/shard_map/ppermute | solution.py:117
  119.4 89.0 %collective-permute-start.7 = (bf16[128,512]{1,0:T(8,128)(2,1)S(1)}, bf16[128,512]{1,0:T(8,128)(2,1)S(1)}, u32[]{:S(2)}, u32[]{:S(2)}) collective-permute-start(bf16[128,512]{1,0:T(8,128)(2,1)S(1)} %get-tuple-element.19), channel_id=1, source_target_pairs={{0,6},{2,4},{4,2},{6,0},{8,14},{10,12},{12,10},{14,8},{1,7},{3,5},... | collective-permute-start | bytes 393224 | tf_op jit(solution)/shard_map/ppermute | solution.py:117
  153.7 16.8 %collective-permute-start.12 = (bf16[128,2048]{1,0:T(8,128)(2,1)S(1)}, bf16[128,2048]{1,0:T(8,128)(2,1)S(1)}, u32[]{:S(2)}, u32[]{:S(2)}) collective-permute-start(bf16[128,2048]{1,0:T(8,128)(2,1)S(1)} %convolution_convert_fusion.11), channel_id=1, source_target_pairs={{4,0},{6,2},{8,12},{10,14},{5,1},{7,3},{9,13},{11,15},{20,16},{22,... | collective-permute-start | bytes 1572872 | tf_op jit(solution)/shard_map/ppermute | solution.py:123
  155.4 44.2 %collective-permute-start.11 = (bf16[128,4096]{1,0:T(8,128)(2,1)S(1)}, bf16[128,4096]{1,0:T(8,128)(2,1)S(1)}, u32[]{:S(2)}, u32[]{:S(2)}) collective-permute-start(bf16[128,4096]{1,0:T(8,128)(2,1)S(1)} %convolution_convert_fusion.2), channel_id=1, source_target_pairs={{0,2},{2,0},{4,6},{6,4},{8,10},{10,8},{12,14},{14,12},{1,3},{3,1},... | collective-permute-start | bytes 3145736 | tf_op jit(solution)/shard_map/ppermute | solution.py:117
  157.1 25.4 %collective-permute-start.13 = (bf16[128,2048]{1,0:T(8,128)(2,1)S(1)}, bf16[128,2048]{1,0:T(8,128)(2,1)S(1)}, u32[]{:S(2)}, u32[]{:S(2)}) collective-permute-start(bf16[128,2048]{1,0:T(8,128)(2,1)S(1)} %convolution_convert_fusion.10), channel_id=1, source_target_pairs={{4,2},{6,0},{8,14},{10,12},{5,3},{7,1},{9,15},{11,13},{20,18},{22,... | collective-permute-start | bytes 1572872 | tf_op jit(solution)/shard_map/ppermute | solution.py:123
  159.5 50.9 %collective-permute-start.19 = (bf16[128,2048]{1,0:T(8,128)(2,1)S(1)}, bf16[128,2048]{1,0:T(8,128)(2,1)S(1)}, u32[]{:S(2)}, u32[]{:S(2)}) collective-permute-start(bf16[128,2048]{1,0:T(8,128)(2,1)S(1)} %convolution_convert_fusion.8), channel_id=1, source_target_pairs={{4,2},{6,0},{8,14},{10,12},{5,3},{7,1},{9,15},{11,13},{20,18},{22,... | collective-permute-start | bytes 1572872 | tf_op jit(solution)/shard_map/ppermute | solution.py:123
  170.4 39.9 %collective-permute-start.18 = (bf16[128,2048]{1,0:T(8,128)(2,1)S(1)}, bf16[128,2048]{1,0:T(8,128)(2,1)S(1)}, u32[]{:S(2)}, u32[]{:S(2)}) collective-permute-start(bf16[128,2048]{1,0:T(8,128)(2,1)S(1)} %convolution_convert_fusion.9), channel_id=1, source_target_pairs={{4,0},{6,2},{8,12},{10,14},{5,1},{7,3},{9,13},{11,15},{20,16},{22,... | collective-permute-start | bytes 1572872 | tf_op jit(solution)/shard_map/ppermute | solution.py:123
  216.1 3.8 %collective-permute-start.20 = (f32[64,256]{1,0:T(8,128)S(1)}, f32[64,256]{1,0:T(8,128)S(1)}, u32[]{:S(2)}, u32[]{:S(2)}) collective-permute-start(f32[64,256]{1,0:T(8,128)S(1)} %add_add_fusion.own_ref), channel_id=1, source_target_pairs={{0,1},{1,0},{2,3},{3,2},{4,5},{5,4},{6,7},{7,6},{8,9},{9,8},{10,11... | collective-permute-start | bytes 196616 | tf_op jit(solution)/shard_map/ppermute | solution.py:83
  216.4 18.2 %collective-permute-start.16 = (bf16[128,512]{1,0:T(8,128)(2,1)S(1)}, bf16[128,512]{1,0:T(8,128)(2,1)S(1)}, u32[]{:S(2)}, u32[]{:S(2)}) collective-permute-start(bf16[128,512]{1,0:T(8,128)(2,1)S(1)} %get-tuple-element.18), channel_id=1, source_target_pairs={{0,8},{2,10},{4,12},{6,14},{8,0},{10,2},{12,4},{14,6},{1,9},{3,11}... | collective-permute-start | bytes 393224 | tf_op jit(solution)/shard_map/ppermute | solution.py:117
  216.4 21.7 %collective-permute-start.17 = (bf16[128,512]{1,0:T(8,128)(2,1)S(1)}, bf16[128,512]{1,0:T(8,128)(2,1)S(1)}, u32[]{:S(2)}, u32[]{:S(2)}) collective-permute-start(bf16[128,512]{1,0:T(8,128)(2,1)S(1)} %get-tuple-element.17), channel_id=1, source_target_pairs={{0,10},{2,8},{4,14},{6,12},{8,2},{10,0},{12,6},{14,4},{1,11},{3,9}... | collective-permute-start | bytes 393224 | tf_op jit(solution)/shard_map/ppermute | solution.py:117
  220.7 17.4 %collective-permute-start.21 = (bf16[128,512]{1,0:T(8,128)(2,1)S(1)}, bf16[128,512]{1,0:T(8,128)(2,1)S(1)}, u32[]{:S(2)}, u32[]{:S(2)}) collective-permute-start(bf16[128,512]{1,0:T(8,128)(2,1)S(1)} %get-tuple-element.23), channel_id=1, source_target_pairs={{0,12},{2,14},{4,8},{6,10},{8,4},{10,6},{12,0},{14,2},{1,13},{3,15... | collective-permute-start | bytes 393224 | tf_op jit(solution)/shard_map/ppermute | solution.py:117
  223.8 14.4 %collective-permute-start.22 = (bf16[128,512]{1,0:T(8,128)(2,1)S(1)}, bf16[128,512]{1,0:T(8,128)(2,1)S(1)}, u32[]{:S(2)}, u32[]{:S(2)}) collective-permute-start(bf16[128,512]{1,0:T(8,128)(2,1)S(1)} %get-tuple-element.24), channel_id=1, source_target_pairs={{0,14},{2,12},{4,10},{6,8},{8,6},{10,4},{12,2},{14,0},{1,15},{3,13... | collective-permute-start | bytes 393224 | tf_op jit(solution)/shard_map/ppermute | solution.py:117
  (4 other events, 29.7 us)
Sparse Core Ops, SparseCore 0:
  22.8 9.9 reduce-scatter.1

commit v2 on v1

v2 whole, which is shorter than its diff:
```python
import functools

import jax
import jax.numpy as jnp
from jax import lax
from jax.experimental import pallas as pl
from jax.experimental.pallas import tpu as pltpu
from jax.sharding import PartitionSpec as P

SLOTS_A_STEP = 8
VMEM_BYTES = 20 * 1024 * 1024
LAST = (((1,), (1,)), ((), ()))
FIRST = (((0,), (0,)), ((), ()))


def ranks_kernel(layout, rank, held_ref, *refs):
    pieces = refs[: len(layout)]
    slot_ref, factors_ref, out_ref, rows_ref = refs[len(layout) :]
    step = pl.program_id(0)
    slots = factors_ref.shape[0] // rank

    @pl.when(step == 0)
    def _():
        out_ref[...] = jnp.zeros_like(out_ref)

    @pl.when((held_ref[0] != 0) & (step == 0))
    def _():
        for (row, column), piece in zip(layout, pieces):
            height, width = piece.shape
            rows_ref[row : row + height, column : column + width] = piece[...]

    @pl.when(held_ref[0] != 0)
    def _():
        products = lax.dot_general(
            factors_ref[...], rows_ref[...], LAST, preferred_element_type=jnp.float32
        )
        slot_of_row = slot_ref[...]
        kept = out_ref[...]
        for slot in range(slots):
            kept = jnp.where(
                slot_of_row == step * slots + slot, products[slot * rank : (slot + 1) * rank], kept
            )
        out_ref[...] = kept


def picked_ranks(pieces, slots, factors, rank, column_block=0, held=True):
    total_rows = slots.shape[0]
    width = max(column + piece.shape[1] for _, column, piece in pieces)
    height = SLOTS_A_STEP * rank
    whole = lambda step, held: (0, 0)
    grid_spec = pltpu.PrefetchScalarGridSpec(
        num_scalar_prefetch=1,
        grid=(factors.shape[0] // height,),
        in_specs=[pl.BlockSpec(piece.shape, whole) for _, _, piece in pieces]
        + [
            pl.BlockSpec((1, total_rows), whole),
            pl.BlockSpec((height, width), lambda step, held: (step * held[0], column_block)),
        ],
        out_specs=pl.BlockSpec((rank, total_rows), whole),
        scratch_shapes=[pltpu.VMEM((total_rows, width), jnp.bfloat16)],
    )
    return pl.pallas_call(
        functools.partial(ranks_kernel, [(row, column) for row, column, _ in pieces], rank),
        grid_spec=grid_spec,
        out_shape=jax.ShapeDtypeStruct((rank, total_rows), jnp.float32),
        compiler_params=pltpu.CompilerParams(vmem_limit_bytes=VMEM_BYTES),
        cost_estimate=pl.CostEstimate(flops=0, bytes_accessed=0, transcendentals=0),
    )(
        jnp.asarray(held, jnp.int32)[None],
        *[piece for _, _, piece in pieces],
        slots[None, :],
        factors,
    )


def updates_kernel(own_ref, peer_ref, slot_ref, factors_ref, out_ref):
    rank = own_ref.shape[0]
    low = (own_ref[...] + peer_ref[...]).astype(jnp.bfloat16).astype(jnp.float32)
    slot_of_row = slot_ref[...]
    spread = jnp.concatenate(
        [
            jnp.where(slot_of_row == slot, low, 0.0).astype(jnp.bfloat16)
            for slot in range(factors_ref.shape[0] // rank)
        ],
        axis=0,
    )
    out_ref[...] = lax.dot_general(
        spread, factors_ref[...], FIRST, preferred_element_type=jnp.float32
    ).astype(out_ref.dtype)


def other_core(value):
    return lax.ppermute(value, "tensor", [(0, 1), (1, 0)])


def row_updates(partial_low, slots, factors):
    other = other_core(partial_low)
    rows, columns = slots.shape[0], factors.shape[1]
    return pl.pallas_call(
        updates_kernel,
        out_shape=jax.ShapeDtypeStruct((rows, columns), jnp.bfloat16),
        in_specs=[pl.BlockSpec(memory_space=pltpu.VMEM)] * 4,
        out_specs=pl.BlockSpec(memory_space=pltpu.VMEM),
        compiler_params=pltpu.CompilerParams(vmem_limit_bytes=VMEM_BYTES),
        cost_estimate=pl.CostEstimate(flops=0, bytes_accessed=0, transcendentals=0),
    )(partial_low, other, slots[None, :], factors)


def looked_up(ids, table):
    hits = ids[..., None] == jnp.arange(table.shape[0], dtype=jnp.int32)
    return jnp.sum(jnp.where(hits, table, 0), axis=-1)


def after(value, *others):
    return lax.optimization_barrier((value, *others))[0]


def line_relay(hidden, base_of, down, up, own_ids, table, rank):
    row_count, width = hidden.shape
    resident = down.shape[0] // rank
    capacity = 4 * row_count // lax.axis_size("dp")
    half = width // 2
    me = lax.axis_index("dp")
    devices = range(8)

    def exchange(value, flip):
        return lax.ppermute(value, "dp", [(i, i ^ flip) for i in devices])

    def middle(value):
        return lax.ppermute(value, "dp", [(i, i ^ 6) for i in devices if i // 2 in (1, 2)])

    def outward(value, flip=0):
        return lax.ppermute(value, "dp", [(i, i ^ 2 ^ flip) for i in devices if i // 2 in (1, 2)])

    one, mid = exchange(hidden, 2), middle(hidden)

    place = {}

    def route(slots, pairs):
        rows = jnp.stack([slots[source] // resident for source, _ in pairs])
        hit = rows == jnp.stack([me ^ owner for _, owner in pairs])[:, None]
        places = jnp.where(hit, jnp.cumsum(hit.astype(jnp.int32), axis=1) - 1, -1)
        place.update({pair: places[n] for n, pair in enumerate(pairs)})

    order = jnp.arange(capacity, dtype=jnp.int32)[:, None]

    def one_hot(place):
        return (order == place[None, :]).astype(jnp.bfloat16)

    def compact(place, piece):
        return jnp.dot(one_hot(place), piece, preferred_element_type=jnp.float32).astype(
            jnp.bfloat16
        )

    def middle_across(value):
        return lax.ppermute(value, "dp", [(i, i ^ 1) for i in devices if i // 2 in (1, 2)])

    def split_rows(source, rows, *earlier, move=lambda value: exchange(value, 1)):
        pair = compact(after(place[source, 1], *earlier), rows)
        mine = compact(after(place[source, 0], pair), rows)
        return [(0, 0, mine), (capacity, 0, move(pair))]

    own_slots = looked_up(own_ids, table)[None, :]
    route(own_slots, [(0, owner) for owner in devices])
    rows_0 = split_rows(0, hidden)
    ids = jnp.broadcast_to(after(own_ids, rows_0[0][2]), (8, 1, row_count))
    ids = lax.all_to_all(ids, "dp", 0, 0, tiled=True)

    edge = (me // 2 == 0) | (me // 2 == 3)
    two_edge, two_middle = outward(mid), middle(one)

    own_slots = other_core(after(own_slots, one, mid, rows_0[1][2]))
    ids = after(ids, own_slots).reshape(2, 2, 2, row_count)
    for axis, bit in enumerate((4, 2, 1)):
        ids = jnp.where(me & bit != 0, jnp.flip(ids, axis), ids)
    slots = looked_up(ids.reshape(8, row_count), table)
    slots = jnp.concatenate([own_slots, slots[1:]])
    route(
        slots,
        [(1, 0), (2, 0), (2, 1), (3, 0), (4, 0), (4, 1), (4, 2), (4, 3), (5, 0), (6, 0), (6, 1), (7, 0)],
    )
    local = slots % resident

    def compact_slots(source):
        return jnp.concatenate(
            [
                jnp.sum(jnp.where(order == place[f, 0][None, :], local[f][None, :] + 1, 0), axis=1) - 1
                for f in (source, source ^ 1)
            ]
        )

    rows_1 = split_rows(2, one)
    slots_0, slots_1, slots_2, slots_3 = (compact_slots(source) for source in (0, 2, 4, 6))
    rows_mid = split_rows(6, mid, rows_1[0][2], move=middle_across)
    base = base_of(rows_mid[0][2])
    low_0 = picked_ranks(rows_0, after(slots_0, rows_mid[0][2]), down, rank)
    update_0 = row_updates(low_0, slots_0, up)
    back = {0: update_0[:capacity], 1: exchange(update_0[capacity:], 1)}
    low_1 = picked_ranks(rows_1, after(slots_1, low_0), down, rank)

    straight = compact(after(place[4, 2], low_1), two_middle)
    two = jnp.where(edge, two_edge, two_middle)
    pair = compact(after(place[4, 1], straight), two)
    update_1 = row_updates(after(low_1, pair), slots_1, up)
    across = compact(after(place[4, 3], update_1), two_middle)
    mine = compact(after(place[4, 0], across), two)
    rows_2 = [(0, 0, mine), (capacity, 0, exchange(pair, 1))]
    rows_3 = [(0, 0, outward(straight)), (capacity, 0, outward(across, 1))]

    low_2 = picked_ranks(rows_2, after(slots_2, mine), down, rank)
    update_2 = row_updates(low_2, slots_2, up)
    early = after(update_1, update_2)
    back[2], back[3] = exchange(early[:capacity], 2), exchange(early[capacity:], 3)
    back[4], back[5] = exchange(update_2[:capacity], 4), exchange(update_2[capacity:], 5)

    low_mid = picked_ranks(rows_mid, after(slots_3, update_2), down, rank, 0, ~edge)
    low_3 = picked_ranks(rows_3, after(slots_3, low_mid), down, rank, 0, edge)
    low_3 = after(low_mid + low_3, back[2], back[3], back[4], back[5])
    update_3 = row_updates(low_3, slots_3, up)
    back[6], back[7] = exchange(update_3[:capacity], 6), exchange(update_3[capacity:], 7)

    def spread_back(owners, *others):
        return lax.dot_general(
            jnp.concatenate([one_hot(place[0, owner]) for owner in owners]),
            jnp.concatenate([after(back[owner], *others) for owner in owners]),
            FIRST,
            preferred_element_type=jnp.float32,
        )

    return base + (spread_back(range(6), update_3) + spread_back((6, 7)))


def all_to_all_relay(hidden, base_of, down, up, own_ids, table, rank):
    row_count = hidden.shape[0]
    peers = lax.axis_size("dp")
    resident = down.shape[0] // rank
    capacity = 4 * row_count // peers
    own_slots = looked_up(own_ids, table)
    hits = (own_slots // resident)[:, None] == jnp.arange(peers, dtype=jnp.int32)[None, :]
    place = jnp.sum(jnp.cumsum(hits.astype(jnp.int32), axis=0) * hits, axis=1) - 1
    target = (own_slots // resident) * capacity + place
    picks = jnp.arange(peers * capacity, dtype=jnp.int32)[:, None] == target[None, :]
    outgoing = jnp.dot(
        picks.astype(jnp.bfloat16), hidden, preferred_element_type=jnp.float32
    ).astype(jnp.bfloat16)
    outgoing_slots = jnp.sum(
        jnp.where(picks, (own_slots % resident)[None, :].astype(jnp.float32) + 1.0, 0.0), axis=1
    ) - 1.0

    def swap(value):
        return lax.all_to_all(
            value.reshape((peers, capacity) + value.shape[1:]), "dp", 0, 0, tiled=True
        ).reshape((peers * capacity,) + value.shape[1:])

    rows = swap(outgoing)
    slots = swap(outgoing_slots).astype(jnp.int32)
    ranks = lax.dot_general(rows, down, LAST, preferred_element_type=jnp.float32)
    selector = slots[:, None] == jnp.arange(resident, dtype=jnp.int32)[None, :]
    low = jnp.sum(
        jnp.where(selector[:, :, None], ranks.reshape(-1, resident, rank), 0.0), axis=1
    )
    low = (low + lax.ppermute(low, "tensor", [(0, 1), (1, 0)])).astype(jnp.bfloat16)
    spread = jnp.where(selector[:, :, None], low[:, None, :], jnp.zeros((), jnp.bfloat16))
    update = jnp.dot(
        spread.reshape(-1, resident * rank), up, preferred_element_type=jnp.float32
    ).astype(jnp.bfloat16)
    return base_of(rows) + swap(update)[target].astype(jnp.float32)


def on_device(
    normed_hidden_states,
    value_base_matrix,
    down_factor_slots,
    up_factor_slots,
    row_adapter_index,
    adapter_slot_table,
):
    resident, rank, width = down_factor_slots.shape

    def base_of(*earlier):
        matrix = after(value_base_matrix, *earlier)
        partial_sum = jnp.dot(normed_hidden_states, matrix, preferred_element_type=jnp.float32)
        return lax.psum_scatter(partial_sum, "tensor", scatter_dimension=1, tiled=True)

    relay = line_relay if lax.axis_size("dp") == 8 else all_to_all_relay
    return relay(
        normed_hidden_states,
        base_of,
        down_factor_slots.reshape(resident * rank, width),
        up_factor_slots.reshape(resident * rank, -1),
        row_adapter_index,
        adapter_slot_table,
        rank,
    ).astype(jnp.bfloat16)


def solution(mesh):
    placed = (
        P(("groups", "dp"), "tensor"),
        P("tensor", None),
        P(("groups", "dp"), None, "tensor"),
        P(("groups", "dp"), None, "tensor"),
        P(("groups", "dp")),
        P("groups"),
    )
    return jax.shard_map(
        on_device,
        mesh=mesh,
        in_specs=placed,
        out_specs=P(("groups", "dp"), "tensor"),
        check_vma=False,
    )
```

time: 251 us -> 201 us (0.80); the launches traced: 247 us -> 201 us
  waiting for transfers between devices: 127 us -> 79 us
  Pallas kernels: 49 us -> 27 us
  matrix products: 14.7 us -> 27.2 us
  local copies, waits for them, and re-layouts: 2.39 us -> 14 us
    ppermute x12 -> x11, waiting for transfers between devices: 104 us -> 53.6 us  [exchange(): return lax.ppermute(value, 'dp', [(i, i ^ flip) for i in devices])]
    pallas_call x6 -> x5, Pallas kernels: 46 us -> 24.1 us  [picked_ranks(): pl.pallas_call(functools.partial(ranks_kernel, [(row, column) for row, co...]
    dot_general x12 -> x10, matrix products: 4.82 us -> 22 us  [compact(): jnp.dot(one_hot(place), piece, preferred_element_type=jnp.float32)]
    unnamed x12 -> x37, local copies, waits for them, and re-layouts: 0.07 us -> 11.7 us
    dot_general x1, matrix products: 7.47 us -> 3.44 us  [base_of(): jnp.dot(normed_hidden_states, matrix, preferred_element_type=jnp.float32)]
    all_to_all x1, starting transfers between devices: 7.28 us -> 4.34 us  [line_relay(): ids = lax.all_to_all(ids, 'dp', 0, 0, tiled=True)]
    ppermute x5 -> x3, starting transfers between devices: 6.62 us -> 4.04 us  [outward(): lax.ppermute(value, 'dp', [(i, i ^ 2 ^ flip) for i in devices if i // 2 i...]
    ppermute x5 -> x3, waiting for transfers between devices: 20.4 us -> 21.8 us  [outward(): lax.ppermute(value, 'dp', [(i, i ^ 2 ^ flip) for i in devices if i // 2 i...]
  transfers between devices with their start and end apart: 25 -> 24, of which waited for: 13 -> 10; matrix products, arithmetic and copies ran while one was open for 7% -> 16% of each run, Pallas kernels for 20% -> 13%
where the time goes in v2:
time: 201 us
  waiting for transfers between devices  79 us (39%)
  starting transfers between devices  34.5 us (17%)
  matrix products  27.2 us (14%)
  Pallas kernels  27 us (13%)
  between operations  14.2 us (7%)
  local copies, waits for them, and re-layouts  14 us (7%)
  other arithmetic  4.52 us (2%)
    ppermute x11, waiting for transfers between devices, exchange(): return lax.ppermute(value, 'dp', [(i, i ^ flip) for i in devices])  53.6 us
    pallas_call x5, Pallas kernels, picked_ranks(): pl.pallas_call(functools.partial(ranks_kernel, [(row, column) for row, co...  24.1 us
    dot_general x10, matrix products, compact(): jnp.dot(one_hot(place), piece, preferred_element_type=jnp.float32)  22 us
    ppermute x3, waiting for transfers between devices, outward(): lax.ppermute(value, 'dp', [(i, i ^ 2 ^ flip) for i in devices if i // 2 i...  21.8 us
    ppermute x11, starting transfers between devices, exchange(): return lax.ppermute(value, 'dp', [(i, i ^ flip) for i in devices])  20 us
    unnamed x37, local copies, waits for them, and re-layouts  11.7 us
    all_to_all x1, starting transfers between devices, line_relay(): ids = lax.all_to_all(ids, 'dp', 0, 0, tiled=True)  4.34 us
    ppermute x3, starting transfers between devices, outward(): lax.ppermute(value, 'dp', [(i, i ^ 2 ^ flip) for i in devices if i // 2 i...  4.04 us
  transfers between devices with their start and end apart: 24, of which 10 were waited for; matrix products, arithmetic and copies ran while one was open for 16% of the time, Pallas kernels for 13%

profile of v2, /device:TPU:0, one launch (start us, length us, event | category | flops | bytes accessed | tf_op | source)
XLA Modules:
  0.0 200.5 jit_solution(11297223650050542828)
XLA Ops:
  6.5 3.0 %collective-permute-start = (bf16[256,4096]{1,0:T(8,128)(2,1)}, bf16[256,4096]{1,0:T(8,128)(2,1)}, u32[]{:S(2)}, u32[]{:S(2)}) collective-permute-start(bf16[256,4096]{1,0:T(8,128)(2,1)} %param.6), channel_id=1, source_target_pairs={{0,4},{2,6},{4,0},{6,2},{8,12},{10,14},{12,8},{14,10},{1,5},{3,7},... | collective-permute-start | bytes 6291464 | tf_op jit(solution)/shard_map/ppermute | solution.py:127
  18.4 4.3 %all-to-all-start = ((s32[8,1,256]{2,1,0:T(1,128)}), s32[8,1,256]{2,1,0:T(1,128)S(1)}, u32[]{:S(2)}, u32[]{:S(2)}) async-start(s32[8,1,256]{2,1,0:T(1,128)} %broadcast_in_dim.151), calls=%async_computation | async-start | bytes 16384 | tf_op jit(solution)/shard_map/all_to_all | solution.py:167
  23.1 17.3 %collective-permute-done.2.refs_1_ = bf16[128,4096]{1,0:T(8,128)(2,1)S(1)} collective-permute-done((bf16[128,4096]{1,0:T(8,128)(2,1)S(1)}, bf16[128,4096]{1,0:T(8,128)(2,1)S(1)}, u32[]{:S(2)}, u32[]{:S(2)}) %collective-permute-start.2) | collective-permute-done | bytes 1048608 | tf_op jit(solution)/shard_map/ppermute | solution.py:127
  40.5 15.1 %collective-permute-done = bf16[256,4096]{1,0:T(8,128)(2,1)} collective-permute-done((bf16[256,4096]{1,0:T(8,128)(2,1)}, bf16[256,4096]{1,0:T(8,128)(2,1)}, u32[]{:S(2)}, u32[]{:S(2)}) %collective-permute-start) | collective-permute-done | bytes 2097184 | tf_op jit(solution)/shard_map/ppermute | solution.py:127
  63.1 3.0 %convolution_convert_fusion.7 = bf16[128,4096]{1,0:T(8,128)(2,1)} fusion(bf16[256,4096]{1,0:T(8,128)(2,1)} %collective-permute-done, s32[256]{0:T(256)S(1)} %bitcast.155), kind=kOutput, calls=%fused_computation.7 | convolution fusion | flops 268992512 | bytes 3146752 | tf_op jit(solution)/shard_map/dot_general | solution.py:151
  66.7 2.2 %convolution_convert_fusion.6.refs_0_ = bf16[128,4096]{1,0:T(8,128)(2,1)S(1)} fusion(bf16[256,4096]{1,0:T(8,128)(2,1)} %collective-permute-done, s32[256]{0:T(256)S(1)} %bitcast.142), kind=kOutput, calls=%fused_computation.6 | convolution fusion | flops 268992512 | bytes 3146752 | tf_op jit(solution)/shard_map/dot_general | solution.py:151
  68.9 3.0 %convolution_convert_fusion.5 = bf16[128,4096]{1,0:T(8,128)(2,1)} fusion(bf16[256,4096]{1,0:T(8,128)(2,1)} %collective-permute-done.1, s32[256]{0:T(256)S(1)} %bitcast.154), kind=kOutput, calls=%fused_computation.5 | convolution fusion | flops 268992512 | bytes 3146752 | tf_op jit(solution)/shard_map/dot_general | solution.py:151
  76.1 5.8 %copy-done = bf16[32,64,4096]{2,1,0:T(8,128)(2,1)S(1)} copy-done((bf16[32,64,4096]{2,1,0:T(8,128)(2,1)S(1)}, bf16[32,64,4096]{2,1,0:T(8,128)(2,1)}, u32[]{:S(2)}) %copy-start) | copy-done | bytes 16777240
  81.8 5.4 %shard_map.64.own_ref = f32[64,256]{1,0:T(8,128)S(1)} custom-call(s32[1]{0:T(128)} %constant.153.clone.1.held_ref, bf16[128,4096]{1,0:T(8,128)(2,1)S(1)} %convolution_convert_fusion.8.refs_0_, bf16[128,4096]{1,0:T(8,128)(2,1)S(1)} %copy-done.4, s32[1,256]{1,0:T(1,128)S(1)} %bitcast.117, bf16[2048,4096]{1,0:T(8,128)(2,1)S(1)} %bitcast.103), custom_call_target="tpu_custom_call" | custom-call | tf_op jit(solution)/shard_map/pallas_call | solution.py:62
  87.4 3.4 %convolution_bitcast_fusion = f32[256,1024]{0,1:T(8,128)} fusion(bf16[4096,1024]{1,0:T(8,128)(2,1)S(1)} %bitcast.173, bf16[256,4096]{1,0:T(8,128)(2,1)S(1)} %copy-done.6), kind=kOutput, calls=%fused_computation.13 | convolution fusion | flops 2147483648 | bytes 11534336 | tf_op jit(solution)/shard_map/dot_general | solution.py:282
  91.3 5.8 %copy-done.1 = bf16[32,64,4096]{2,1,0:T(8,128)(2,1)S(1)} copy-done((bf16[32,64,4096]{2,1,0:T(8,128)(2,1)S(1)}, bf16[32,64,4096]{2,1,0:T(8,128)(2,1)}, u32[]{:S(2)}) %copy-start.1) | copy-done | bytes 16777240
  97.1 6.7 %shard_map.66.own_ref = f32[64,256]{1,0:T(8,128)S(1)} custom-call(s32[1]{0:T(128)} %constant.153.clone.1.held_ref, bf16[128,4096]{1,0:T(8,128)(2,1)S(1)} %convolution_convert_fusion.6.refs_0_, bf16[128,4096]{1,0:T(8,128)(2,1)} %collective-permute-done.6.refs_1_, s32[1,256]{1,0:T(1,128)S(1)} %bitcast.119, bf16[2048,4096]{1,0:T(8,128)(2,1)S(1)} %bitcast.104), custom_call_target="tpu_custom_call" | custom-call | tf_op jit(solution)/shard_map/pallas_call | solution.py:62
  103.8 2.3 %convolution_convert_fusion.3 = bf16[128,4096]{1,0:T(8,128)(2,1)S(1)} fusion(bf16[256,4096]{1,0:T(8,128)(2,1)} %collective-permute-done.7, s32[256]{0:T(256)S(1)} %bitcast.151), kind=kOutput, calls=%fused_computation.3 | convolution fusion | flops 268992512 | bytes 3146752 | tf_op jit(solution)/shard_map/dot_general | solution.py:151
  106.1 5.5 %collective-permute-done.8 = bf16[256,4096]{1,0:T(8,128)(2,1)} collective-permute-done((bf16[256,4096]{1,0:T(8,128)(2,1)}, bf16[256,4096]{1,0:T(8,128)(2,1)}, u32[]{:S(2)}, u32[]{:S(2)}) %collective-permute-start.8) | collective-permute-done | bytes 2097184 | tf_op jit(solution)/shard_map/ppermute | solution.py:133
  111.7 2.2 %convolution_convert_fusion.2 = bf16[128,4096]{1,0:T(8,128)(2,1)S(1)} fusion(bf16[256,4096]{1,0:T(8,128)(2,1)} %collective-permute-done.8, bf16[256,4096]{1,0:T(8,128)(2,1)} %collective-permute-done.7, pred[]{:T(512)S(6)} %or.3, s32[256]{0:T(256)S(1)} %bitcast.150), kind=kOutput, calls=%fused_computation.2 | convolution fusion | flops 270041088 | bytes 5243905 | tf_op jit(solution)/shard_map/dot_general | solution.py:151
  117.9 2.4 %convolution_convert_fusion.1 = bf16[128,4096]{1,0:T(8,128)(2,1)S(1)} fusion(bf16[256,4096]{1,0:T(8,128)(2,1)} %collective-permute-done.7, s32[256]{0:T(256)S(1)} %bitcast.149), kind=kOutput, calls=%fused_computation.1 | convolution fusion | flops 268992512 | bytes 3146752 | tf_op jit(solution)/shard_map/dot_general | solution.py:151
  121.6 2.2 %convolution_convert_fusion.refs_0_ = bf16[128,4096]{1,0:T(8,128)(2,1)S(1)} fusion(bf16[256,4096]{1,0:T(8,128)(2,1)} %collective-permute-done.8, bf16[256,4096]{1,0:T(8,128)(2,1)} %collective-permute-done.7, pred[]{:T(512)S(6)} %or.3, s32[256]{0:T(256)S(1)} %bitcast.139), kind=kOutput, calls=%fused_computation | convolution fusion | flops 270041088 | bytes 5243905 | tf_op jit(solution)/shard_map/dot_general | solution.py:151
  123.8 14.9 %collective-permute-done.10.refs_1_ = bf16[128,4096]{1,0:T(8,128)(2,1)S(1)} collective-permute-done((bf16[128,4096]{1,0:T(8,128)(2,1)S(1)}, bf16[128,4096]{1,0:T(8,128)(2,1)S(1)}, u32[]{:S(2)}, u32[]{:S(2)}) %collective-permute-start.10) | collective-permute-done | bytes 1048608 | tf_op jit(solution)/shard_map/ppermute | solution.py:127
  138.7 5.4 %shard_map.68.own_ref = f32[64,256]{1,0:T(8,128)S(1)} custom-call(s32[1]{0:T(128)} %constant.153.clone.1.held_ref, bf16[128,4096]{1,0:T(8,128)(2,1)S(1)} %convolution_convert_fusion.refs_0_, bf16[128,4096]{1,0:T(8,128)(2,1)S(1)} %collective-permute-done.10.refs_1_, s32[1,256]{1,0:T(1,128)S(1)} %bitcast.121, bf16[2048,4096]{1,0:T(8,128)(2,1)S(1)} %bitcast.107), custom_call_target="tpu_custom_call" | custom-call | tf_op jit(solution)/shard_map/pallas_call | solution.py:62
  146.2 4.0 %collective-permute-start.14 = (bf16[128,512]{1,0:T(8,128)(2,1)S(1)}, bf16[128,512]{1,0:T(8,128)(2,1)S(1)}, u32[]{:S(2)}, u32[]{:S(2)}) collective-permute-start(bf16[128,512]{1,0:T(8,128)(2,1)S(1)} %get-tuple-element.64), channel_id=1, source_target_pairs={{0,4},{2,6},{4,0},{6,2},{8,12},{10,14},{12,8},{14,10},{1,5},{3,7},... | collective-permute-start | bytes 393224 | tf_op jit(solution)/shard_map/ppermute | solution.py:127
  155.5 16.3 %collective-permute-done.13.refs_1_ = bf16[128,4096]{1,0:T(8,128)(2,1)S(1)} collective-permute-done((bf16[128,4096]{1,0:T(8,128)(2,1)S(1)}, bf16[128,4096]{1,0:T(8,128)(2,1)S(1)}, u32[]{:S(2)}, u32[]{:S(2)}) %collective-permute-start.13) | collective-permute-done | bytes 1048608 | tf_op jit(solution)/shard_map/ppermute | solution.py:133
  173.3 5.4 %shard_map.71 = f32[64,256]{1,0:T(8,128)S(1)} custom-call(s32[1]{0:T(128)} %bitcast.67.held_ref, bf16[128,4096]{1,0:T(8,128)(2,1)S(1)} %collective-permute-done.12.refs_0_, bf16[128,4096]{1,0:T(8,128)(2,1)S(1)} %collective-permute-done.13.refs_1_, s32[1,256]{1,0:T(1,128)S(1)} %bitcast.115, bf16[2048,4096]{1,0:T(8,128)(2,1)S(1)} %bitcast.109), custom_call_target="tpu_custom_call" | custom-call | tf_op jit(solution)/shard_map/pallas_call | solution.py:62
  182.1 2.5 %collective-permute-start.21 = (bf16[128,512]{1,0:T(8,128)(2,1)S(1)}, bf16[128,512]{1,0:T(8,128)(2,1)S(1)}, u32[]{:S(2)}, u32[]{:S(2)}) collective-permute-start(bf16[128,512]{1,0:T(8,128)(2,1)S(1)} %get-tuple-element.60), channel_id=1, source_target_pairs={{0,14},{2,12},{4,10},{6,8},{8,6},{10,4},{12,2},{14,0},{1,15},{3,13... | collective-permute-start | bytes 393224 | tf_op jit(solution)/shard_map/ppermute | solution.py:127
  184.7 4.4 %collective-permute-done.20 = bf16[128,512]{1,0:T(8,128)(2,1)S(1)} collective-permute-done((bf16[128,512]{1,0:T(8,128)(2,1)S(1)}, bf16[128,512]{1,0:T(8,128)(2,1)S(1)}, u32[]{:S(2)}, u32[]{:S(2)}) %collective-permute-start.20) | collective-permute-done | bytes 131104 | tf_op jit(solution)/shard_map/ppermute | solution.py:127
  (152 shorter events, 44.0 us)
Async XLA Ops:
  6.5 49.0 %collective-permute-start = (bf16[256,4096]{1,0:T(8,128)(2,1)}, bf16[256,4096]{1,0:T(8,128)(2,1)}, u32[]{:S(2)}, u32[]{:S(2)}) collective-permute-start(bf16[256,4096]{1,0:T(8,128)(2,1)} %param.6), channel_id=1, source_target_pairs={{0,4},{2,6},{4,0},{6,2},{8,12},{10,14},{12,8},{14,10},{1,5},{3,7},... | collective-permute-start | bytes 6291464 | tf_op jit(solution)/shard_map/ppermute | solution.py:127
  9.6 46.0 %collective-permute-start.1 = (bf16[256,4096]{1,0:T(8,128)(2,1)}, bf16[256,4096]{1,0:T(8,128)(2,1)}, u32[]{:S(2)}, u32[]{:S(2)}) collective-permute-start(bf16[256,4096]{1,0:T(8,128)(2,1)} %param.6), channel_id=1, source_target_pairs={{4,8},{6,10},{8,4},{10,6},{5,9},{7,11},{9,5},{11,7},{20,24},{22,26... | collective-permute-start | bytes 6291464 | tf_op jit(solution)/shard_map/ppermute | solution.py:130
  15.8 24.7 %collective-permute-start.2 = (bf16[128,4096]{1,0:T(8,128)(2,1)S(1)}, bf16[128,4096]{1,0:T(8,128)(2,1)S(1)}, u32[]{:S(2)}, u32[]{:S(2)}) collective-permute-start(bf16[128,4096]{1,0:T(8,128)(2,1)S(1)} %convolution_convert_fusion.9), channel_id=1, source_target_pairs={{0,2},{2,0},{4,6},{6,4},{8,10},{10,8},{12,14},{14,12},{1,3},{3,1},... | collective-permute-start | bytes 3145736 | tf_op jit(solution)/shard_map/ppermute | solution.py:127
  18.4 42.3 %all-to-all-start = ((s32[8,1,256]{2,1,0:T(1,128)}), s32[8,1,256]{2,1,0:T(1,128)S(1)}, u32[]{:S(2)}, u32[]{:S(2)}) async-start(s32[8,1,256]{2,1,0:T(1,128)} %broadcast_in_dim.151), calls=%async_computation | async-start | bytes 16384 | tf_op jit(solution)/shard_map/all_to_all | solution.py:167
  22.8 168.6 %reduce-scatter.2.cloned.1.call-start = ((), (), s32[]{:S(2)}) async-start(), calls=%async_computation.2 | async-start | bytes 1572864 | tf_op jit(solution)/shard_map/reduce_scatter | solution.py:283
  55.5 5.2 %collective-permute-start.3 = (s32[1,256]{1,0:T(1,128)S(1)}, s32[1,256]{1,0:T(1,128)S(1)}, u32[]{:S(2)}, u32[]{:S(2)}) collective-permute-start(s32[1,256]{1,0:T(1,128)S(1)} %bitcast.148), channel_id=1, source_target_pairs={{0,1},{1,0},{2,3},{3,2},{4,5},{5,4},{6,7},{7,6},{8,9},{9,8},{10,11... | collective-permute-start | bytes 3080 | tf_op jit(solution)/shard_map/ppermute | solution.py:93
  55.5 48.3 %collective-permute-start.7 = (bf16[256,4096]{1,0:T(8,128)(2,1)}, bf16[256,4096]{1,0:T(8,128)(2,1)}, u32[]{:S(2)}, u32[]{:S(2)}) collective-permute-start(bf16[256,4096]{1,0:T(8,128)(2,1)} %collective-permute-done), channel_id=1, source_target_pairs={{4,8},{6,10},{8,4},{10,6},{5,9},{7,11},{9,5},{11,7},{20,24},{22,26... | collective-permute-start | bytes 6291464 | tf_op jit(solution)/shard_map/ppermute | solution.py:130
  57.5 54.1 %collective-permute-start.8 = (bf16[256,4096]{1,0:T(8,128)(2,1)}, bf16[256,4096]{1,0:T(8,128)(2,1)}, u32[]{:S(2)}, u32[]{:S(2)}) collective-permute-start(bf16[256,4096]{1,0:T(8,128)(2,1)} %collective-permute-done.1), channel_id=1, source_target_pairs={{4,0},{6,2},{8,12},{10,14},{5,1},{7,3},{9,13},{11,15},{20,16},{22,... | collective-permute-start | bytes 6291464 | tf_op jit(solution)/shard_map/ppermute | solution.py:133
  66.2 25.1 %collective-permute-start.6 = (bf16[128,4096]{1,0:T(8,128)(2,1)}, bf16[128,4096]{1,0:T(8,128)(2,1)}, u32[]{:S(2)}, u32[]{:S(2)}) collective-permute-start(bf16[128,4096]{1,0:T(8,128)(2,1)} %convolution_convert_fusion.7), channel_id=1, source_target_pairs={{0,2},{2,0},{4,6},{6,4},{8,10},{10,8},{12,14},{14,12},{1,3},{3,1},... | collective-permute-start | bytes 3145736 | tf_op jit(solution)/shard_map/ppermute | solution.py:127
  72.0 79.3 %collective-permute-start.5 = (bf16[128,4096]{1,0:T(8,128)(2,1)}, bf16[128,4096]{1,0:T(8,128)(2,1)}, u32[]{:S(2)}, u32[]{:S(2)}) collective-permute-start(bf16[128,4096]{1,0:T(8,128)(2,1)} %convolution_convert_fusion.5), channel_id=1, source_target_pairs={{4,6},{6,4},{8,10},{10,8},{5,7},{7,5},{9,11},{11,9},{20,22},{22,20... | collective-permute-start | bytes 3145736 | tf_op jit(solution)/shard_map/ppermute | solution.py:156
  87.2 57.0 %collective-permute-start.4 = (f32[64,256]{1,0:T(8,128)S(1)}, f32[64,256]{1,0:T(8,128)S(1)}, u32[]{:S(2)}, u32[]{:S(2)}) collective-permute-start(f32[64,256]{1,0:T(8,128)S(1)} %shard_map.64.own_ref), channel_id=1, source_target_pairs={{0,1},{1,0},{2,3},{3,2},{4,5},{5,4},{6,7},{7,6},{8,9},{9,8},{10,11... | collective-permute-start | bytes 196616 | tf_op jit(solution)/shard_map/ppermute | solution.py:93
  113.9 24.8 %collective-permute-start.10 = (bf16[128,4096]{1,0:T(8,128)(2,1)S(1)}, bf16[128,4096]{1,0:T(8,128)(2,1)S(1)}, u32[]{:S(2)}, u32[]{:S(2)}) collective-permute-start(bf16[128,4096]{1,0:T(8,128)(2,1)S(1)} %convolution_convert_fusion.2), channel_id=1, source_target_pairs={{0,2},{2,0},{4,6},{6,4},{8,10},{10,8},{12,14},{14,12},{1,3},{3,1},... | collective-permute-start | bytes 3145736 | tf_op jit(solution)/shard_map/ppermute | solution.py:127
  115.6 1.6 collective-permute-start.9
  115.7 37.3 %collective-permute-start.12 = (bf16[128,4096]{1,0:T(8,128)(2,1)S(1)}, bf16[128,4096]{1,0:T(8,128)(2,1)S(1)}, u32[]{:S(2)}, u32[]{:S(2)}) collective-permute-start(bf16[128,4096]{1,0:T(8,128)(2,1)S(1)} %convolution_convert_fusion.3), channel_id=1, source_target_pairs={{4,0},{6,2},{8,12},{10,14},{5,1},{7,3},{9,13},{11,15},{20,16},{22,... | collective-permute-start | bytes 3145736 | tf_op jit(solution)/shard_map/ppermute | solution.py:133
  120.3 51.4 %collective-permute-start.13 = (bf16[128,4096]{1,0:T(8,128)(2,1)S(1)}, bf16[128,4096]{1,0:T(8,128)(2,1)S(1)}, u32[]{:S(2)}, u32[]{:S(2)}) collective-permute-start(bf16[128,4096]{1,0:T(8,128)(2,1)S(1)} %convolution_convert_fusion.1), channel_id=1, source_target_pairs={{4,2},{6,0},{8,14},{10,12},{5,3},{7,1},{9,15},{11,13},{20,18},{22,... | collective-permute-start | bytes 3145736 | tf_op jit(solution)/shard_map/ppermute | solution.py:133
  144.1 1.3 collective-permute-start.11
  146.2 32.4 %collective-permute-start.14 = (bf16[128,512]{1,0:T(8,128)(2,1)S(1)}, bf16[128,512]{1,0:T(8,128)(2,1)S(1)}, u32[]{:S(2)}, u32[]{:S(2)}) collective-permute-start(bf16[128,512]{1,0:T(8,128)(2,1)S(1)} %get-tuple-element.64), channel_id=1, source_target_pairs={{0,4},{2,6},{4,0},{6,2},{8,12},{10,14},{12,8},{14,10},{1,5},{3,7},... | collective-permute-start | bytes 393224 | tf_op jit(solution)/shard_map/ppermute | solution.py:127
  150.2 28.5 %collective-permute-start.15 = (bf16[128,512]{1,0:T(8,128)(2,1)S(1)}, bf16[128,512]{1,0:T(8,128)(2,1)S(1)}, u32[]{:S(2)}, u32[]{:S(2)}) collective-permute-start(bf16[128,512]{1,0:T(8,128)(2,1)S(1)} %get-tuple-element.63), channel_id=1, source_target_pairs={{0,6},{2,4},{4,2},{6,0},{8,14},{10,12},{12,10},{14,8},{1,7},{3,5},... | collective-permute-start | bytes 393224 | tf_op jit(solution)/shard_map/ppermute | solution.py:127
  151.3 27.4 %collective-permute-start.16 = (bf16[128,512]{1,0:T(8,128)(2,1)S(1)}, bf16[128,512]{1,0:T(8,128)(2,1)S(1)}, u32[]{:S(2)}, u32[]{:S(2)}) collective-permute-start(bf16[128,512]{1,0:T(8,128)(2,1)S(1)} %get-tuple-element.62), channel_id=1, source_target_pairs={{0,8},{2,10},{4,12},{6,14},{8,0},{10,2},{12,4},{14,6},{1,9},{3,11}... | collective-permute-start | bytes 393224 | tf_op jit(solution)/shard_map/ppermute | solution.py:127
  153.0 25.7 %collective-permute-start.17 = (bf16[128,512]{1,0:T(8,128)(2,1)S(1)}, bf16[128,512]{1,0:T(8,128)(2,1)S(1)}, u32[]{:S(2)}, u32[]{:S(2)}) collective-permute-start(bf16[128,512]{1,0:T(8,128)(2,1)S(1)} %get-tuple-element.61), channel_id=1, source_target_pairs={{0,10},{2,8},{4,14},{6,12},{8,2},{10,0},{12,6},{14,4},{1,11},{3,9}... | collective-permute-start | bytes 393224 | tf_op jit(solution)/shard_map/ppermute | solution.py:127
  171.7 9.0 %collective-permute-start.19 = (bf16[128,512]{1,0:T(8,128)(2,1)S(1)}, bf16[128,512]{1,0:T(8,128)(2,1)S(1)}, u32[]{:S(2)}, u32[]{:S(2)}) collective-permute-start(bf16[128,512]{1,0:T(8,128)(2,1)S(1)} %get-tuple-element.57), channel_id=1, source_target_pairs={{0,2},{2,0},{4,6},{6,4},{8,10},{10,8},{12,14},{14,12},{1,3},{3,1},... | collective-permute-start | bytes 393224 | tf_op jit(solution)/shard_map/ppermute | solution.py:127
  178.7 1.3 collective-permute-start.18
  180.8 8.3 %collective-permute-start.20 = (bf16[128,512]{1,0:T(8,128)(2,1)S(1)}, bf16[128,512]{1,0:T(8,128)(2,1)S(1)}, u32[]{:S(2)}, u32[]{:S(2)}) collective-permute-start(bf16[128,512]{1,0:T(8,128)(2,1)S(1)} %get-tuple-element.59), channel_id=1, source_target_pairs={{0,12},{2,14},{4,8},{6,10},{8,4},{10,6},{12,0},{14,2},{1,13},{3,15... | collective-permute-start | bytes 393224 | tf_op jit(solution)/shard_map/ppermute | solution.py:127
  182.1 8.9 %collective-permute-start.21 = (bf16[128,512]{1,0:T(8,128)(2,1)S(1)}, bf16[128,512]{1,0:T(8,128)(2,1)S(1)}, u32[]{:S(2)}, u32[]{:S(2)}) collective-permute-start(bf16[128,512]{1,0:T(8,128)(2,1)S(1)} %get-tuple-element.60), channel_id=1, source_target_pairs={{0,14},{2,12},{4,10},{6,8},{8,6},{10,4},{12,2},{14,0},{1,15},{3,13... | collective-permute-start | bytes 393224 | tf_op jit(solution)/shard_map/ppermute | solution.py:127
  (15 other events, 277.9 us)
Sparse Core Ops, SparseCore 0:
  91.0 14.0 reduce-scatter.1

commit v3 on v2

--- a/solution.py
+++ b/solution.py
@@ -106,6 +106,26 @@
     )(partial_low, other, slots[None, :], factors)
 
 
+def base_kernel(rows_ref, matrix_ref, out_ref):
+    out_ref[...] = jnp.dot(rows_ref[...], matrix_ref[...], preferred_element_type=jnp.float32)
+
+
+def base_product(rows, matrix):
+    block = matrix.shape[1] // 4
+    return pl.pallas_call(
+        base_kernel,
+        grid=(4,),
+        out_shape=jax.ShapeDtypeStruct((rows.shape[0], matrix.shape[1]), jnp.float32),
+        in_specs=[
+            pl.BlockSpec(rows.shape, lambda step: (0, 0)),
+            pl.BlockSpec((matrix.shape[0], block), lambda step: (0, step)),
+        ],
+        out_specs=pl.BlockSpec((rows.shape[0], block), lambda step: (0, step)),
+        compiler_params=pltpu.CompilerParams(vmem_limit_bytes=VMEM_BYTES),
+        cost_estimate=pl.CostEstimate(flops=0, bytes_accessed=0, transcendentals=0),
+    )(rows, matrix)
+
+
 def looked_up(ids, table):
     hits = ids[..., None] == jnp.arange(table.shape[0], dtype=jnp.int32)
     return jnp.sum(jnp.where(hits, table, 0), axis=-1)
@@ -115,7 +135,7 @@
     return lax.optimization_barrier((value, *others))[0]
 
 
-def line_relay(hidden, base_of, down, up, own_ids, table, rank):
+def line_relay(hidden, matrix, down, up, own_ids, table, rank):
     row_count, width = hidden.shape
     resident = down.shape[0] // rank
     capacity = 4 * row_count // lax.axis_size("dp")
@@ -166,10 +186,13 @@
     ids = jnp.broadcast_to(after(own_ids, rows_0[0][2]), (8, 1, row_count))
     ids = lax.all_to_all(ids, "dp", 0, 0, tiled=True)
 
+    partial_base = base_product(hidden, after(matrix, rows_0[0][2]))
+    base = lax.psum_scatter(partial_base, "tensor", scatter_dimension=1, tiled=True)
+
     edge = (me // 2 == 0) | (me // 2 == 3)
     two_edge, two_middle = outward(mid), middle(one)
 
-    own_slots = other_core(after(own_slots, one, mid, rows_0[1][2]))
+    own_slots = other_core(after(own_slots, one, mid, rows_0[1][2], partial_base))
     ids = after(ids, own_slots).reshape(2, 2, 2, row_count)
     for axis, bit in enumerate((4, 2, 1)):
         ids = jnp.where(me & bit != 0, jnp.flip(ids, axis), ids)
@@ -192,10 +215,9 @@
     rows_1 = split_rows(2, one)
     slots_0, slots_1, slots_2, slots_3 = (compact_slots(source) for source in (0, 2, 4, 6))
     rows_mid = split_rows(6, mid, rows_1[0][2], move=middle_across)
-    base = base_of(rows_mid[0][2])
     low_0 = picked_ranks(rows_0, after(slots_0, rows_mid[0][2]), down, rank)
     update_0 = row_updates(low_0, slots_0, up)
-    back = {0: update_0[:capacity], 1: exchange(update_0[capacity:], 1)}
+    back = {0: update_0[:capacity]}
     low_1 = picked_ranks(rows_1, after(slots_1, low_0), down, rank)
 
     straight = compact(after(place[4, 2], low_1), two_middle)
@@ -209,13 +231,14 @@
 
     low_2 = picked_ranks(rows_2, after(slots_2, mine), down, rank)
     update_2 = row_updates(low_2, slots_2, up)
+    back[1] = exchange(after(update_0, update_2)[capacity:], 1)
     early = after(update_1, update_2)
     back[2], back[3] = exchange(early[:capacity], 2), exchange(early[capacity:], 3)
     back[4], back[5] = exchange(update_2[:capacity], 4), exchange(update_2[capacity:], 5)
 
     low_mid = picked_ranks(rows_mid, after(slots_3, update_2), down, rank, 0, ~edge)
     low_3 = picked_ranks(rows_3, after(slots_3, low_mid), down, rank, 0, edge)
-    low_3 = after(low_mid + low_3, back[2], back[3], back[4], back[5])
+    low_3 = after(low_mid + low_3, back[1], back[2], back[3], back[4], back[5])
     update_3 = row_updates(low_3, slots_3, up)
     back[6], back[7] = exchange(update_3[:capacity], 6), exchange(update_3[capacity:], 7)
 
@@ -230,7 +253,7 @@
     return base + (spread_back(range(6), update_3) + spread_back((6, 7)))
 
 
-def all_to_all_relay(hidden, base_of, down, up, own_ids, table, rank):
+def all_to_all_relay(hidden, matrix, down, up, own_ids, table, rank):
     row_count = hidden.shape[0]
     peers = lax.axis_size("dp")
     resident = down.shape[0] // rank
@@ -264,7 +287,9 @@
     update = jnp.dot(
         spread.reshape(-1, resident * rank), up, preferred_element_type=jnp.float32
     ).astype(jnp.bfloat16)
-    return base_of(rows) + swap(update)[target].astype(jnp.float32)
+    base = jnp.dot(hidden, matrix, preferred_element_type=jnp.float32)
+    base = lax.psum_scatter(base, "tensor", scatter_dimension=1, tiled=True)
+    return base + swap(update)[target].astype(jnp.float32)
 
 
 def on_device(
@@ -277,15 +302,10 @@
 ):
     resident, rank, width = down_factor_slots.shape
 
-    def base_of(*earlier):
-        matrix = after(value_base_matrix, *earlier)
-        partial_sum = jnp.dot(normed_hidden_states, matrix, preferred_element_type=jnp.float32)
-        return lax.psum_scatter(partial_sum, "tensor", scatter_dimension=1, tiled=True)
-
     relay = line_relay if lax.axis_size("dp") == 8 else all_to_all_relay
     return relay(
         normed_hidden_states,
-        base_of,
+        value_base_matrix,
         down_factor_slots.reshape(resident * rank, width),
         up_factor_slots.reshape(resident * rank, -1),
         row_adapter_index,

time: 201 us -> 200 us (level)
  waiting for transfers between devices: 79 us -> 90.3 us
  matrix products: 27.2 us -> 19.3 us
  starting transfers between devices: 34.5 us -> 29.5 us
  Pallas kernels: 27 us -> 29.9 us
  local copies, waits for them, and re-layouts: 14 us -> 11.8 us
    ppermute x3, waiting for transfers between devices: 21.8 us -> 33.5 us  [outward(): lax.ppermute(value, 'dp', [(i, i ^ 2 ^ flip) for i in devices if i // 2 i...]
    dot_general x10, matrix products: 22 us -> 16.9 us  [compact(): jnp.dot(one_hot(place), piece, preferred_element_type=jnp.float32)]
    pallas_call x0 -> x1, Pallas kernels: none -> 4 us  [base_product(): pl.pallas_call(base_kernel, grid=(4,), out_shape=jax.ShapeDtypeStruct((ro...]
    dot_general x1 -> x0, matrix products: 3.44 us -> none  [base_of(): jnp.dot(normed_hidden_states, matrix, preferred_element_type=jnp.float32)]
    ppermute x11, starting transfers between devices: 20 us -> 17.3 us  [exchange(): return lax.ppermute(value, 'dp', [(i, i ^ flip) for i in devices])]
    unnamed x37 -> x31, local copies, waits for them, and re-layouts: 11.7 us -> 10.2 us
  transfers between devices with their start and end apart: 24 -> 24, of which waited for: 10 -> 12; matrix products, arithmetic and copies ran while one was open for 16% -> 12% of each run, Pallas kernels for 13% -> 15%
where the time goes in v3:
time: 200 us; the launch traced here: 199 us
  waiting for transfers between devices  90.3 us (45%)
  Pallas kernels  29.9 us (15%)
  starting transfers between devices  29.5 us (15%)
  matrix products  19.3 us (10%)
  between operations  14.1 us (7%)
  local copies, waits for them, and re-layouts  11.8 us (6%)
  other arithmetic  4.52 us (2%)
    ppermute x11, waiting for transfers between devices, exchange(): return lax.ppermute(value, 'dp', [(i, i ^ flip) for i in devices])  52.2 us
    ppermute x3, waiting for transfers between devices, outward(): lax.ppermute(value, 'dp', [(i, i ^ 2 ^ flip) for i in devices if i // 2 i...  33.5 us
    pallas_call x5, Pallas kernels, picked_ranks(): pl.pallas_call(functools.partial(ranks_kernel, [(row, column) for row, co...  22.9 us
    ppermute x11, starting transfers between devices, exchange(): return lax.ppermute(value, 'dp', [(i, i ^ flip) for i in devices])  17.3 us
    dot_general x10, matrix products, compact(): jnp.dot(one_hot(place), piece, preferred_element_type=jnp.float32)  16.9 us
    unnamed x31, local copies, waits for them, and re-layouts  10.2 us
    all_to_all x1, starting transfers between devices, line_relay(): ids = lax.all_to_all(ids, 'dp', 0, 0, tiled=True)  4.35 us
    ppermute x3, starting transfers between devices, outward(): lax.ppermute(value, 'dp', [(i, i ^ 2 ^ flip) for i in devices if i // 2 i...  4.19 us
  transfers between devices with their start and end apart: 24, of which 12 were waited for; matrix products, arithmetic and copies ran while one was open for 12% of the time, Pallas kernels for 15%

profile of v3, /device:TPU:0, one launch (start us, length us, event | category | flops | bytes accessed | tf_op | source)
XLA Modules:
  0.0 199.4 jit_solution(11682706799333346060)
XLA Ops:
  6.5 3.0 %collective-permute-start.1 = (bf16[256,4096]{1,0:T(8,128)(2,1)}, bf16[256,4096]{1,0:T(8,128)(2,1)}, u32[]{:S(2)}, u32[]{:S(2)}) collective-permute-start(bf16[256,4096]{1,0:T(8,128)(2,1)} %rows_ref.1), channel_id=1, source_target_pairs={{0,4},{2,6},{4,0},{6,2},{8,12},{10,14},{12,8},{14,10},{1,5},{3,7},... | collective-permute-start | bytes 6291464 | tf_op jit(solution)/shard_map/ppermute | solution.py:147
  13.5 3.0 %convolution_convert_fusion.9 = bf16[128,4096]{1,0:T(8,128)(2,1)} fusion(bf16[256,4096]{1,0:T(8,128)(2,1)} %rows_ref.1, s32[256]{0:T(256)S(1)} %bitcast.132), kind=kOutput, calls=%fused_computation.9 | convolution fusion | flops 268992512 | bytes 3146752 | tf_op jit(solution)/shard_map/dot_general | solution.py:171
  19.2 4.4 %all-to-all-start = ((s32[8,1,256]{2,1,0:T(1,128)}), s32[8,1,256]{2,1,0:T(1,128)S(1)}, u32[]{:S(2)}, u32[]{:S(2)}) async-start(s32[8,1,256]{2,1,0:T(1,128)} %broadcast_in_dim.152), calls=%async_computation.1 | async-start | bytes 16384 | tf_op jit(solution)/shard_map/all_to_all | solution.py:187
  23.6 3.4 %copy-done.3 = bf16[4096,1024]{1,0:T(8,128)(2,1)S(1)} copy-done((bf16[4096,1024]{1,0:T(8,128)(2,1)S(1)}, bf16[4096,1024]{1,0:T(8,128)(2,1)}, u32[]{:S(2)}) %copy-start.3) | copy-done | bytes 8388632
  26.9 4.0 %shard_map.64 = f32[256,1024]{1,0:T(8,128)S(1)} custom-call(bf16[256,4096]{1,0:T(8,128)(2,1)S(1)} %copy-done.2, bf16[4096,1024]{1,0:T(8,128)(2,1)S(1)} %copy-done.3), custom_call_target="tpu_custom_call" | custom-call | tf_op jit(solution)/shard_map/pallas_call | solution.py:115
  32.3 9.2 %collective-permute-done.refs_1_ = bf16[128,4096]{1,0:T(8,128)(2,1)} collective-permute-done((bf16[128,4096]{1,0:T(8,128)(2,1)}, bf16[128,4096]{1,0:T(8,128)(2,1)}, u32[]{:S(2)}, u32[]{:S(2)}) %collective-permute-start) | collective-permute-done | bytes 1048608 | tf_op jit(solution)/shard_map/ppermute | solution.py:147
  41.5 14.1 %collective-permute-done.1 = bf16[256,4096]{1,0:T(8,128)(2,1)} collective-permute-done((bf16[256,4096]{1,0:T(8,128)(2,1)}, bf16[256,4096]{1,0:T(8,128)(2,1)}, u32[]{:S(2)}, u32[]{:S(2)}) %collective-permute-start.1) | collective-permute-done | bytes 2097184 | tf_op jit(solution)/shard_map/ppermute | solution.py:147
  57.7 3.0 %all-to-all-done = s32[8,1,256]{2,1,0:T(1,128)S(1)} async-done(((s32[8,1,256]{2,1,0:T(1,128)}), s32[8,1,256]{2,1,0:T(1,128)S(1)}, u32[]{:S(2)}, u32[]{:S(2)}) %all-to-all-start) | async-done | bytes 8224 | tf_op jit(solution)/shard_map/all_to_all | solution.py:187
  72.8 5.8 %copy-done = bf16[32,64,4096]{2,1,0:T(8,128)(2,1)S(1)} copy-done((bf16[32,64,4096]{2,1,0:T(8,128)(2,1)S(1)}, bf16[32,64,4096]{2,1,0:T(8,128)(2,1)}, u32[]{:S(2)}) %copy-start) | copy-done | bytes 16777240
  78.6 6.6 %shard_map.65.own_ref = f32[64,256]{1,0:T(8,128)S(1)} custom-call(s32[1]{0:T(128)} %constant.153.clone.1.held_ref, bf16[128,4096]{1,0:T(8,128)(2,1)S(1)} %convolution_convert_fusion.8.refs_0_, bf16[128,4096]{1,0:T(8,128)(2,1)} %collective-permute-done.refs_1_, s32[1,256]{1,0:T(1,128)S(1)} %bitcast.113, bf16[2048,4096]{1,0:T(8,128)(2,1)S(1)} %bitcast.99), custom_call_target="tpu_custom_call" | custom-call | tf_op jit(solution)/shard_map/pallas_call | solution.py:62
  85.8 3.0 %collective-permute-done.6.refs_1_ = bf16[128,4096]{1,0:T(8,128)(2,1)S(1)} collective-permute-done((bf16[128,4096]{1,0:T(8,128)(2,1)S(1)}, bf16[128,4096]{1,0:T(8,128)(2,1)S(1)}, u32[]{:S(2)}, u32[]{:S(2)}) %collective-permute-start.6) | collective-permute-done | bytes 1048608 | tf_op jit(solution)/shard_map/ppermute | solution.py:147
  88.8 5.4 %shard_map.67.own_ref = f32[64,256]{1,0:T(8,128)S(1)} custom-call(s32[1]{0:T(128)} %constant.153.clone.1.held_ref, bf16[128,4096]{1,0:T(8,128)(2,1)S(1)} %convolution_convert_fusion.6.refs_0_, bf16[128,4096]{1,0:T(8,128)(2,1)S(1)} %collective-permute-done.6.refs_1_, s32[1,256]{1,0:T(1,128)S(1)} %bitcast.115, bf16[2048,4096]{1,0:T(8,128)(2,1)S(1)} %bitcast.100), custom_call_target="tpu_custom_call" | custom-call | tf_op jit(solution)/shard_map/pallas_call | solution.py:62
  94.6 17.0 %collective-permute-done.8 = bf16[256,4096]{1,0:T(8,128)(2,1)} collective-permute-done((bf16[256,4096]{1,0:T(8,128)(2,1)}, bf16[256,4096]{1,0:T(8,128)(2,1)}, u32[]{:S(2)}, u32[]{:S(2)}) %collective-permute-start.8) | collective-permute-done | bytes 2097184 | tf_op jit(solution)/shard_map/ppermute | solution.py:153
  119.7 2.2 %convolution_convert_fusion.refs_0_ = bf16[128,4096]{1,0:T(8,128)(2,1)S(1)} fusion(bf16[256,4096]{1,0:T(8,128)(2,1)} %collective-permute-done.8, bf16[256,4096]{1,0:T(8,128)(2,1)S(1)} %collective-permute-done.7, pred[]{:T(512)S(6)} %or.3, s32[256]{0:T(256)S(1)} %bitcast.135), kind=kOutput, calls=%fused_computation | convolution fusion | flops 270041088 | bytes 5243905 | tf_op jit(solution)/shard_map/dot_general | solution.py:171
  121.9 16.8 %collective-permute-done.10.refs_1_ = bf16[128,4096]{1,0:T(8,128)(2,1)S(1)} collective-permute-done((bf16[128,4096]{1,0:T(8,128)(2,1)S(1)}, bf16[128,4096]{1,0:T(8,128)(2,1)S(1)}, u32[]{:S(2)}, u32[]{:S(2)}) %collective-permute-start.10) | collective-permute-done | bytes 1048608 | tf_op jit(solution)/shard_map/ppermute | solution.py:147
  138.7 5.4 %shard_map.69.own_ref = f32[64,256]{1,0:T(8,128)S(1)} custom-call(s32[1]{0:T(128)} %constant.153.clone.1.held_ref, bf16[128,4096]{1,0:T(8,128)(2,1)S(1)} %convolution_convert_fusion.refs_0_, bf16[128,4096]{1,0:T(8,128)(2,1)S(1)} %collective-permute-done.10.refs_1_, s32[1,256]{1,0:T(1,128)S(1)} %bitcast.117, bf16[2048,4096]{1,0:T(8,128)(2,1)S(1)} %bitcast.103), custom_call_target="tpu_custom_call" | custom-call | tf_op jit(solution)/shard_map/pallas_call | solution.py:62
  146.2 2.6 %collective-permute-start.15 = (bf16[128,512]{1,0:T(8,128)(2,1)S(1)}, bf16[128,512]{1,0:T(8,128)(2,1)S(1)}, u32[]{:S(2)}, u32[]{:S(2)}) collective-permute-start(bf16[128,512]{1,0:T(8,128)(2,1)S(1)} %get-tuple-element.64), channel_id=1, source_target_pairs={{0,4},{2,6},{4,0},{6,2},{8,12},{10,14},{12,8},{14,10},{1,5},{3,7},... | collective-permute-start | bytes 393224 | tf_op jit(solution)/shard_map/ppermute | solution.py:147
  152.2 16.5 %collective-permute-done.13.refs_1_ = bf16[128,4096]{1,0:T(8,128)(2,1)S(1)} collective-permute-done((bf16[128,4096]{1,0:T(8,128)(2,1)S(1)}, bf16[128,4096]{1,0:T(8,128)(2,1)S(1)}, u32[]{:S(2)}, u32[]{:S(2)}) %collective-permute-start.13) | collective-permute-done | bytes 1048608 | tf_op jit(solution)/shard_map/ppermute | solution.py:153
  168.9 5.4 %shard_map.72 = f32[64,256]{1,0:T(8,128)S(1)} custom-call(s32[1]{0:T(128)} %bitcast.66.held_ref, bf16[128,4096]{1,0:T(8,128)(2,1)S(1)} %collective-permute-done.12.refs_0_, bf16[128,4096]{1,0:T(8,128)(2,1)S(1)} %collective-permute-done.13.refs_1_, s32[1,256]{1,0:T(1,128)S(1)} %bitcast.111, bf16[2048,4096]{1,0:T(8,128)(2,1)S(1)} %bitcast.105), custom_call_target="tpu_custom_call" | custom-call | tf_op jit(solution)/shard_map/pallas_call | solution.py:62
  174.3 2.7 %collective-permute-done.18 = bf16[128,512]{1,0:T(8,128)(2,1)S(1)} collective-permute-done((bf16[128,512]{1,0:T(8,128)(2,1)S(1)}, bf16[128,512]{1,0:T(8,128)(2,1)S(1)}, u32[]{:S(2)}, u32[]{:S(2)}) %collective-permute-start.18) | collective-permute-done | bytes 131104 | tf_op jit(solution)/shard_map/ppermute | solution.py:147
  179.1 2.2 %collective-permute-start.20 = (bf16[128,512]{1,0:T(8,128)(2,1)S(1)}, bf16[128,512]{1,0:T(8,128)(2,1)S(1)}, u32[]{:S(2)}, u32[]{:S(2)}) collective-permute-start(bf16[128,512]{1,0:T(8,128)(2,1)S(1)} %get-tuple-element.59), channel_id=1, source_target_pairs={{0,12},{2,14},{4,8},{6,10},{8,4},{10,6},{12,0},{14,2},{1,13},{3,15... | collective-permute-start | bytes 393224 | tf_op jit(solution)/shard_map/ppermute | solution.py:147
  181.3 2.4 %collective-permute-start.21 = (bf16[128,512]{1,0:T(8,128)(2,1)S(1)}, bf16[128,512]{1,0:T(8,128)(2,1)S(1)}, u32[]{:S(2)}, u32[]{:S(2)}) collective-permute-start(bf16[128,512]{1,0:T(8,128)(2,1)S(1)} %get-tuple-element.60), channel_id=1, source_target_pairs={{0,14},{2,12},{4,10},{6,8},{8,6},{10,4},{12,2},{14,0},{1,15},{3,13... | collective-permute-start | bytes 393224 | tf_op jit(solution)/shard_map/ppermute | solution.py:147
  183.8 3.6 %collective-permute-done.20 = bf16[128,512]{1,0:T(8,128)(2,1)S(1)} collective-permute-done((bf16[128,512]{1,0:T(8,128)(2,1)S(1)}, bf16[128,512]{1,0:T(8,128)(2,1)S(1)}, u32[]{:S(2)}, u32[]{:S(2)}) %collective-permute-start.20) | collective-permute-done | bytes 131104 | tf_op jit(solution)/shard_map/ppermute | solution.py:147
  187.4 2.7 %collective-permute-done.21 = bf16[128,512]{1,0:T(8,128)(2,1)S(1)} collective-permute-done((bf16[128,512]{1,0:T(8,128)(2,1)S(1)}, bf16[128,512]{1,0:T(8,128)(2,1)S(1)}, u32[]{:S(2)}, u32[]{:S(2)}) %collective-permute-start.21) | collective-permute-done | bytes 131104 | tf_op jit(solution)/shard_map/ppermute | solution.py:147
  (146 shorter events, 41.0 us)
Async XLA Ops:
  6.5 49.1 %collective-permute-start.1 = (bf16[256,4096]{1,0:T(8,128)(2,1)}, bf16[256,4096]{1,0:T(8,128)(2,1)}, u32[]{:S(2)}, u32[]{:S(2)}) collective-permute-start(bf16[256,4096]{1,0:T(8,128)(2,1)} %rows_ref.1), channel_id=1, source_target_pairs={{0,4},{2,6},{4,0},{6,2},{8,12},{10,14},{12,8},{14,10},{1,5},{3,7},... | collective-permute-start | bytes 6291464 | tf_op jit(solution)/shard_map/ppermute | solution.py:147
  9.6 46.0 %collective-permute-start.2 = (bf16[256,4096]{1,0:T(8,128)(2,1)}, bf16[256,4096]{1,0:T(8,128)(2,1)}, u32[]{:S(2)}, u32[]{:S(2)}) collective-permute-start(bf16[256,4096]{1,0:T(8,128)(2,1)} %rows_ref.1), channel_id=1, source_target_pairs={{4,8},{6,10},{8,4},{10,6},{5,9},{7,11},{9,5},{11,7},{20,24},{22,26... | collective-permute-start | bytes 6291464 | tf_op jit(solution)/shard_map/ppermute | solution.py:150
  16.6 24.9 %collective-permute-start = (bf16[128,4096]{1,0:T(8,128)(2,1)}, bf16[128,4096]{1,0:T(8,128)(2,1)}, u32[]{:S(2)}, u32[]{:S(2)}) collective-permute-start(bf16[128,4096]{1,0:T(8,128)(2,1)} %convolution_convert_fusion.9), channel_id=1, source_target_pairs={{0,2},{2,0},{4,6},{6,4},{8,10},{10,8},{12,14},{14,12},{1,3},{3,1},... | collective-permute-start | bytes 3145736 | tf_op jit(solution)/shard_map/ppermute | solution.py:147
  19.2 41.5 %all-to-all-start = ((s32[8,1,256]{2,1,0:T(1,128)}), s32[8,1,256]{2,1,0:T(1,128)S(1)}, u32[]{:S(2)}, u32[]{:S(2)}) async-start(s32[8,1,256]{2,1,0:T(1,128)} %broadcast_in_dim.152), calls=%async_computation.1 | async-start | bytes 16384 | tf_op jit(solution)/shard_map/all_to_all | solution.py:187
  23.5 166.9 %reduce-scatter.2.cloned.1.call-start = ((), (), s32[]{:S(2)}) async-start(), calls=%async_computation.2 | async-start | bytes 1572864 | tf_op jit(solution)/shard_map/reduce_scatter | solution.py:190
  55.6 5.1 %collective-permute-start.3 = (s32[1,256]{1,0:T(1,128)S(1)}, s32[1,256]{1,0:T(1,128)S(1)}, u32[]{:S(2)}, u32[]{:S(2)}) collective-permute-start(s32[1,256]{1,0:T(1,128)S(1)} %bitcast.144), channel_id=1, source_target_pairs={{0,1},{1,0},{2,3},{3,2},{4,5},{5,4},{6,7},{7,6},{8,9},{9,8},{10,11... | collective-permute-start | bytes 3080 | tf_op jit(solution)/shard_map/ppermute | solution.py:93
  55.6 38.5 %collective-permute-start.7 = (bf16[256,4096]{1,0:T(8,128)(2,1)}, bf16[256,4096]{1,0:T(8,128)(2,1)S(1)}, u32[]{:S(2)}, u32[]{:S(2)}) collective-permute-start(bf16[256,4096]{1,0:T(8,128)(2,1)} %collective-permute-done.1), channel_id=1, source_target_pairs={{4,8},{6,10},{8,4},{10,6},{5,9},{7,11},{9,5},{11,7},{20,24},{22,26... | collective-permute-start | bytes 6291464 | tf_op jit(solution)/shard_map/ppermute | solution.py:150
  56.4 55.3 %collective-permute-start.8 = (bf16[256,4096]{1,0:T(8,128)(2,1)}, bf16[256,4096]{1,0:T(8,128)(2,1)}, u32[]{:S(2)}, u32[]{:S(2)}) collective-permute-start(bf16[256,4096]{1,0:T(8,128)(2,1)} %collective-permute-done.2), channel_id=1, source_target_pairs={{4,0},{6,2},{8,12},{10,14},{5,1},{7,3},{9,13},{11,15},{20,16},{22,... | collective-permute-start | bytes 6291464 | tf_op jit(solution)/shard_map/ppermute | solution.py:153
  65.0 23.8 %collective-permute-start.6 = (bf16[128,4096]{1,0:T(8,128)(2,1)S(1)}, bf16[128,4096]{1,0:T(8,128)(2,1)S(1)}, u32[]{:S(2)}, u32[]{:S(2)}) collective-permute-start(bf16[128,4096]{1,0:T(8,128)(2,1)S(1)} %convolution_convert_fusion.7), channel_id=1, source_target_pairs={{0,2},{2,0},{4,6},{6,4},{8,10},{10,8},{12,14},{14,12},{1,3},{3,1},... | collective-permute-start | bytes 3145736 | tf_op jit(solution)/shard_map/ppermute | solution.py:147
  69.8 80.2 %collective-permute-start.5 = (bf16[128,4096]{1,0:T(8,128)(2,1)S(1)}, bf16[128,4096]{1,0:T(8,128)(2,1)S(1)}, u32[]{:S(2)}, u32[]{:S(2)}) collective-permute-start(bf16[128,4096]{1,0:T(8,128)(2,1)S(1)} %convolution_convert_fusion.5), channel_id=1, source_target_pairs={{4,6},{6,4},{8,10},{10,8},{5,7},{7,5},{9,11},{11,9},{20,22},{22,20... | collective-permute-start | bytes 3145736 | tf_op jit(solution)/shard_map/ppermute | solution.py:176
  85.2 59.1 %collective-permute-start.4 = (f32[64,256]{1,0:T(8,128)S(1)}, f32[64,256]{1,0:T(8,128)S(1)}, u32[]{:S(2)}, u32[]{:S(2)}) collective-permute-start(f32[64,256]{1,0:T(8,128)S(1)} %shard_map.65.own_ref), channel_id=1, source_target_pairs={{0,1},{1,0},{2,3},{3,2},{4,5},{5,4},{6,7},{7,6},{8,9},{9,8},{10,11... | collective-permute-start | bytes 196616 | tf_op jit(solution)/shard_map/ppermute | solution.py:93
  113.9 24.8 %collective-permute-start.10 = (bf16[128,4096]{1,0:T(8,128)(2,1)S(1)}, bf16[128,4096]{1,0:T(8,128)(2,1)S(1)}, u32[]{:S(2)}, u32[]{:S(2)}) collective-permute-start(bf16[128,4096]{1,0:T(8,128)(2,1)S(1)} %convolution_convert_fusion.2), channel_id=1, source_target_pairs={{0,2},{2,0},{4,6},{6,4},{8,10},{10,8},{12,14},{14,12},{1,3},{3,1},... | collective-permute-start | bytes 3145736 | tf_op jit(solution)/shard_map/ppermute | solution.py:147
  115.4 1.4 collective-permute-start.9
  115.6 35.0 %collective-permute-start.12 = (bf16[128,4096]{1,0:T(8,128)(2,1)S(1)}, bf16[128,4096]{1,0:T(8,128)(2,1)S(1)}, u32[]{:S(2)}, u32[]{:S(2)}) collective-permute-start(bf16[128,4096]{1,0:T(8,128)(2,1)S(1)} %convolution_convert_fusion.3), channel_id=1, source_target_pairs={{4,0},{6,2},{8,12},{10,14},{5,1},{7,3},{9,13},{11,15},{20,16},{22,... | collective-permute-start | bytes 3145736 | tf_op jit(solution)/shard_map/ppermute | solution.py:153
  118.1 50.6 %collective-permute-start.13 = (bf16[128,4096]{1,0:T(8,128)(2,1)S(1)}, bf16[128,4096]{1,0:T(8,128)(2,1)S(1)}, u32[]{:S(2)}, u32[]{:S(2)}) collective-permute-start(bf16[128,4096]{1,0:T(8,128)(2,1)S(1)} %convolution_convert_fusion.1), channel_id=1, source_target_pairs={{4,2},{6,0},{8,14},{10,12},{5,3},{7,1},{9,15},{11,13},{20,18},{22,... | collective-permute-start | bytes 3145736 | tf_op jit(solution)/shard_map/ppermute | solution.py:153
  144.1 1.3 collective-permute-start.11
  146.2 28.0 %collective-permute-start.15 = (bf16[128,512]{1,0:T(8,128)(2,1)S(1)}, bf16[128,512]{1,0:T(8,128)(2,1)S(1)}, u32[]{:S(2)}, u32[]{:S(2)}) collective-permute-start(bf16[128,512]{1,0:T(8,128)(2,1)S(1)} %get-tuple-element.64), channel_id=1, source_target_pairs={{0,4},{2,6},{4,0},{6,2},{8,12},{10,14},{12,8},{14,10},{1,5},{3,7},... | collective-permute-start | bytes 393224 | tf_op jit(solution)/shard_map/ppermute | solution.py:147
  148.9 25.4 %collective-permute-start.16 = (bf16[128,512]{1,0:T(8,128)(2,1)S(1)}, bf16[128,512]{1,0:T(8,128)(2,1)S(1)}, u32[]{:S(2)}, u32[]{:S(2)}) collective-permute-start(bf16[128,512]{1,0:T(8,128)(2,1)S(1)} %get-tuple-element.63), channel_id=1, source_target_pairs={{0,6},{2,4},{4,2},{6,0},{8,14},{10,12},{12,10},{14,8},{1,7},{3,5},... | collective-permute-start | bytes 393224 | tf_op jit(solution)/shard_map/ppermute | solution.py:147
  149.9 24.4 %collective-permute-start.14 = (bf16[128,512]{1,0:T(8,128)(2,1)S(1)}, bf16[128,512]{1,0:T(8,128)(2,1)S(1)}, u32[]{:S(2)}, u32[]{:S(2)}) collective-permute-start(bf16[128,512]{1,0:T(8,128)(2,1)S(1)} %slice.195), channel_id=1, source_target_pairs={{0,2},{2,0},{4,6},{6,4},{8,10},{10,8},{12,14},{14,12},{1,3},{3,1},... | collective-permute-start | bytes 393224 | tf_op jit(solution)/shard_map/ppermute | solution.py:147
  150.5 23.8 %collective-permute-start.17 = (bf16[128,512]{1,0:T(8,128)(2,1)S(1)}, bf16[128,512]{1,0:T(8,128)(2,1)S(1)}, u32[]{:S(2)}, u32[]{:S(2)}) collective-permute-start(bf16[128,512]{1,0:T(8,128)(2,1)S(1)} %get-tuple-element.62), channel_id=1, source_target_pairs={{0,8},{2,10},{4,12},{6,14},{8,0},{10,2},{12,4},{14,6},{1,9},{3,11}... | collective-permute-start | bytes 393224 | tf_op jit(solution)/shard_map/ppermute | solution.py:147
  168.7 8.4 %collective-permute-start.18 = (bf16[128,512]{1,0:T(8,128)(2,1)S(1)}, bf16[128,512]{1,0:T(8,128)(2,1)S(1)}, u32[]{:S(2)}, u32[]{:S(2)}) collective-permute-start(bf16[128,512]{1,0:T(8,128)(2,1)S(1)} %get-tuple-element.61), channel_id=1, source_target_pairs={{0,10},{2,8},{4,14},{6,12},{8,2},{10,0},{12,6},{14,4},{1,11},{3,9}... | collective-permute-start | bytes 393224 | tf_op jit(solution)/shard_map/ppermute | solution.py:147
  177.1 1.3 collective-permute-start.19
  179.1 8.3 %collective-permute-start.20 = (bf16[128,512]{1,0:T(8,128)(2,1)S(1)}, bf16[128,512]{1,0:T(8,128)(2,1)S(1)}, u32[]{:S(2)}, u32[]{:S(2)}) collective-permute-start(bf16[128,512]{1,0:T(8,128)(2,1)S(1)} %get-tuple-element.59), channel_id=1, source_target_pairs={{0,12},{2,14},{4,8},{6,10},{8,4},{10,6},{12,0},{14,2},{1,13},{3,15... | collective-permute-start | bytes 393224 | tf_op jit(solution)/shard_map/ppermute | solution.py:147
  181.3 8.8 %collective-permute-start.21 = (bf16[128,512]{1,0:T(8,128)(2,1)S(1)}, bf16[128,512]{1,0:T(8,128)(2,1)S(1)}, u32[]{:S(2)}, u32[]{:S(2)}) collective-permute-start(bf16[128,512]{1,0:T(8,128)(2,1)S(1)} %get-tuple-element.60), channel_id=1, source_target_pairs={{0,14},{2,12},{4,10},{6,8},{8,6},{10,4},{12,2},{14,0},{1,15},{3,13... | collective-permute-start | bytes 393224 | tf_op jit(solution)/shard_map/ppermute | solution.py:147
  (13 other events, 284.8 us)
Sparse Core Ops, SparseCore 0:
  32.1 9.8 reduce-scatter.1

commit v4 on v3

--- a/solution.py
+++ b/solution.py
@@ -218,7 +218,7 @@
     low_0 = picked_ranks(rows_0, after(slots_0, rows_mid[0][2]), down, rank)
     update_0 = row_updates(low_0, slots_0, up)
     back = {0: update_0[:capacity]}
-    low_1 = picked_ranks(rows_1, after(slots_1, low_0), down, rank)
+    low_1 = picked_ranks(rows_1, after(slots_1, update_0), down, rank)
 
     straight = compact(after(place[4, 2], low_1), two_middle)
     two = jnp.where(edge, two_edge, two_middle)
@@ -250,7 +250,8 @@
             preferred_element_type=jnp.float32,
         )
 
-    return base + (spread_back(range(6), update_3) + spread_back((6, 7)))
+    early = after(base + spread_back(range(6), update_3), update_3)
+    return early + spread_back((6, 7))
 
 
 def all_to_all_relay(hidden, matrix, down, up, own_ids, table, rank):

time: 200 us -> 198 us (0.990)
  waiting for transfers between devices: 90.3 us -> 81.1 us
  starting transfers between devices: 29.5 us -> 33.6 us
    ppermute x3, waiting for transfers between devices: 33.5 us -> 25.7 us  [outward(): lax.ppermute(value, 'dp', [(i, i ^ 2 ^ flip) for i in devices if i // 2 i...]
    ppermute x11, starting transfers between devices: 17.3 us -> 21.6 us  [exchange(): return lax.ppermute(value, 'dp', [(i, i ^ flip) for i in devices])]
    ppermute x11, waiting for transfers between devices: 52.2 us -> 49.2 us  [exchange(): return lax.ppermute(value, 'dp', [(i, i ^ flip) for i in devices])]
    dot_general x10, matrix products: 16.9 us -> 19 us  [compact(): jnp.dot(one_hot(place), piece, preferred_element_type=jnp.float32)]
    unnamed x31 -> x25, local copies, waits for them, and re-layouts: 10.2 us -> 10.2 us
  transfers between devices with their start and end apart: 24 -> 24, of which waited for: 12 -> 13; matrix products, arithmetic and copies ran while one was open for 12% -> 14% of each run, Pallas kernels for 15% -> 15%
where the time goes in v4:
time: 198 us; the launch traced here: 196 us
  waiting for transfers between devices  81.1 us (41%)
  starting transfers between devices  33.6 us (17%)
  Pallas kernels  30 us (15%)
  matrix products  20.7 us (10%)
  between operations  14.1 us (7%)
  local copies, waits for them, and re-layouts  11.8 us (6%)
  other arithmetic  5.31 us (3%)
    ppermute x11, waiting for transfers between devices, exchange(): return lax.ppermute(value, 'dp', [(i, i ^ flip) for i in devices])  49.2 us
    ppermute x3, waiting for transfers between devices, outward(): lax.ppermute(value, 'dp', [(i, i ^ 2 ^ flip) for i in devices if i // 2 i...  25.7 us
    pallas_call x5, Pallas kernels, picked_ranks(): pl.pallas_call(functools.partial(ranks_kernel, [(row, column) for row, co...  23.1 us
    ppermute x11, starting transfers between devices, exchange(): return lax.ppermute(value, 'dp', [(i, i ^ flip) for i in devices])  21.6 us
    dot_general x10, matrix products, compact(): jnp.dot(one_hot(place), piece, preferred_element_type=jnp.float32)  19 us
    unnamed x25, local copies, waits for them, and re-layouts  10.2 us
    all_to_all x1, starting transfers between devices, line_relay(): ids = lax.all_to_all(ids, 'dp', 0, 0, tiled=True)  4.38 us
    ppermute x3, starting transfers between devices, outward(): lax.ppermute(value, 'dp', [(i, i ^ 2 ^ flip) for i in devices if i // 2 i...  4.05 us
  transfers between devices with their start and end apart: 24, of which 13 were waited for; matrix products, arithmetic and copies ran while one was open for 14% of the time, Pallas kernels for 15%

profile of v4, /device:TPU:0, one launch (start us, length us, event | category | flops | bytes accessed | tf_op | source)
XLA Modules:
  0.0 196.5 jit_solution(16901555659524548565)
XLA Ops:
  6.5 3.0 %collective-permute-start.1 = (bf16[256,4096]{1,0:T(8,128)(2,1)}, bf16[256,4096]{1,0:T(8,128)(2,1)}, u32[]{:S(2)}, u32[]{:S(2)}) collective-permute-start(bf16[256,4096]{1,0:T(8,128)(2,1)} %rows_ref.1), channel_id=1, source_target_pairs={{0,4},{2,6},{4,0},{6,2},{8,12},{10,14},{12,8},{14,10},{1,5},{3,7},... | collective-permute-start | bytes 6291464 | tf_op jit(solution)/shard_map/ppermute | solution.py:147
  13.5 3.0 %convolution_convert_fusion.9 = bf16[128,4096]{1,0:T(8,128)(2,1)} fusion(bf16[256,4096]{1,0:T(8,128)(2,1)} %rows_ref.1, s32[256]{0:T(256)S(1)} %bitcast.130), kind=kOutput, calls=%fused_computation.9 | convolution fusion | flops 268992512 | bytes 3146752 | tf_op jit(solution)/shard_map/dot_general | solution.py:171
  18.5 3.4 %copy-done.4 = bf16[4096,1024]{1,0:T(8,128)(2,1)S(1)} copy-done((bf16[4096,1024]{1,0:T(8,128)(2,1)S(1)}, bf16[4096,1024]{1,0:T(8,128)(2,1)}, u32[]{:S(2)}) %copy-start.4) | copy-done | bytes 8388632
  21.9 4.0 %shard_map.64 = f32[256,1024]{1,0:T(8,128)S(1)} custom-call(bf16[256,4096]{1,0:T(8,128)(2,1)S(1)} %copy-done.3, bf16[4096,1024]{1,0:T(8,128)(2,1)S(1)} %copy-done.4), custom_call_target="tpu_custom_call" | custom-call | tf_op jit(solution)/shard_map/pallas_call | solution.py:115
  27.6 4.4 %all-to-all-start = ((s32[8,1,256]{2,1,0:T(1,128)}), s32[8,1,256]{2,1,0:T(1,128)S(1)}, u32[]{:S(2)}, u32[]{:S(2)}) async-start(s32[8,1,256]{2,1,0:T(1,128)} %broadcast_in_dim.152), calls=%async_computation.1 | async-start | bytes 16384 | tf_op jit(solution)/shard_map/all_to_all | solution.py:187
  32.3 9.2 %collective-permute-done.refs_1_ = bf16[128,4096]{1,0:T(8,128)(2,1)} collective-permute-done((bf16[128,4096]{1,0:T(8,128)(2,1)}, bf16[128,4096]{1,0:T(8,128)(2,1)}, u32[]{:S(2)}, u32[]{:S(2)}) %collective-permute-start) | collective-permute-done | bytes 1048608 | tf_op jit(solution)/shard_map/ppermute | solution.py:147
  41.5 14.1 %collective-permute-done.1 = bf16[256,4096]{1,0:T(8,128)(2,1)} collective-permute-done((bf16[256,4096]{1,0:T(8,128)(2,1)}, bf16[256,4096]{1,0:T(8,128)(2,1)}, u32[]{:S(2)}, u32[]{:S(2)}) %collective-permute-start.1) | collective-permute-done | bytes 2097184 | tf_op jit(solution)/shard_map/ppermute | solution.py:147
  57.7 3.0 %all-to-all-done = s32[8,1,256]{2,1,0:T(1,128)S(1)} async-done(((s32[8,1,256]{2,1,0:T(1,128)}), s32[8,1,256]{2,1,0:T(1,128)S(1)}, u32[]{:S(2)}, u32[]{:S(2)}) %all-to-all-start) | async-done | bytes 8224 | tf_op jit(solution)/shard_map/all_to_all | solution.py:187
  63.0 3.0 %convolution_convert_fusion.7 = bf16[128,4096]{1,0:T(8,128)(2,1)} fusion(bf16[256,4096]{1,0:T(8,128)(2,1)} %collective-permute-done.1, s32[256]{0:T(256)S(1)} %bitcast.149), kind=kOutput, calls=%fused_computation.7 | convolution fusion | flops 268992512 | bytes 3146752 | tf_op jit(solution)/shard_map/dot_general | solution.py:171
  68.6 3.1 %convolution_convert_fusion.5 = bf16[128,4096]{1,0:T(8,128)(2,1)} fusion(bf16[256,4096]{1,0:T(8,128)(2,1)} %collective-permute-done.2, s32[256]{0:T(256)S(1)} %bitcast.148), kind=kOutput, calls=%fused_computation.5 | convolution fusion | flops 268992512 | bytes 3146752 | tf_op jit(solution)/shard_map/dot_general | solution.py:171
  74.8 5.8 %copy-done = bf16[32,64,4096]{2,1,0:T(8,128)(2,1)S(1)} copy-done((bf16[32,64,4096]{2,1,0:T(8,128)(2,1)S(1)}, bf16[32,64,4096]{2,1,0:T(8,128)(2,1)}, u32[]{:S(2)}) %copy-start) | copy-done | bytes 16777240
  80.6 6.8 %shard_map.65.own_ref = f32[64,256]{1,0:T(8,128)S(1)} custom-call(s32[1]{0:T(128)} %constant.153.clone.1.held_ref, bf16[128,4096]{1,0:T(8,128)(2,1)S(1)} %convolution_convert_fusion.8.refs_0_, bf16[128,4096]{1,0:T(8,128)(2,1)} %collective-permute-done.refs_1_, s32[1,256]{1,0:T(1,128)S(1)} %bitcast.113, bf16[2048,4096]{1,0:T(8,128)(2,1)S(1)} %bitcast.99), custom_call_target="tpu_custom_call" | custom-call | tf_op jit(solution)/shard_map/pallas_call | solution.py:62
  89.9 5.4 %shard_map.67.own_ref = f32[64,256]{1,0:T(8,128)S(1)} custom-call(s32[1]{0:T(128)} %constant.153.clone.1.held_ref, bf16[128,4096]{1,0:T(8,128)(2,1)S(1)} %convolution_convert_fusion.6.refs_0_, bf16[128,4096]{1,0:T(8,128)(2,1)S(1)} %collective-permute-done.6.refs_1_, s32[1,256]{1,0:T(1,128)S(1)} %bitcast.111, bf16[2048,4096]{1,0:T(8,128)(2,1)S(1)} %bitcast.100), custom_call_target="tpu_custom_call" | custom-call | tf_op jit(solution)/shard_map/pallas_call | solution.py:62
  95.7 12.6 %collective-permute-done.8 = bf16[256,4096]{1,0:T(8,128)(2,1)} collective-permute-done((bf16[256,4096]{1,0:T(8,128)(2,1)}, bf16[256,4096]{1,0:T(8,128)(2,1)}, u32[]{:S(2)}, u32[]{:S(2)}) %collective-permute-start.8) | collective-permute-done | bytes 2097184 | tf_op jit(solution)/shard_map/ppermute | solution.py:153
  108.3 2.2 %convolution_convert_fusion.2 = bf16[128,4096]{1,0:T(8,128)(2,1)S(1)} fusion(bf16[256,4096]{1,0:T(8,128)(2,1)} %collective-permute-done.8, bf16[256,4096]{1,0:T(8,128)(2,1)S(1)} %collective-permute-done.7, pred[]{:T(512)S(6)} %or.3, s32[256]{0:T(256)S(1)} %bitcast.144), kind=kOutput, calls=%fused_computation.2 | convolution fusion | flops 270041088 | bytes 5243905 | tf_op jit(solution)/shard_map/dot_general | solution.py:171
  116.2 2.2 %convolution_convert_fusion.refs_0_ = bf16[128,4096]{1,0:T(8,128)(2,1)S(1)} fusion(bf16[256,4096]{1,0:T(8,128)(2,1)} %collective-permute-done.8, bf16[256,4096]{1,0:T(8,128)(2,1)S(1)} %collective-permute-done.7, pred[]{:T(512)S(6)} %or.3, s32[256]{0:T(256)S(1)} %bitcast.133), kind=kOutput, calls=%fused_computation | convolution fusion | flops 270041088 | bytes 5243905 | tf_op jit(solution)/shard_map/dot_general | solution.py:171
  118.4 17.1 %collective-permute-done.10.refs_1_ = bf16[128,4096]{1,0:T(8,128)(2,1)S(1)} collective-permute-done((bf16[128,4096]{1,0:T(8,128)(2,1)S(1)}, bf16[128,4096]{1,0:T(8,128)(2,1)S(1)}, u32[]{:S(2)}, u32[]{:S(2)}) %collective-permute-start.10) | collective-permute-done | bytes 1048608 | tf_op jit(solution)/shard_map/ppermute | solution.py:147
  135.5 5.4 %shard_map.69.own_ref = f32[64,256]{1,0:T(8,128)S(1)} custom-call(s32[1]{0:T(128)} %constant.153.clone.1.held_ref, bf16[128,4096]{1,0:T(8,128)(2,1)S(1)} %convolution_convert_fusion.refs_0_, bf16[128,4096]{1,0:T(8,128)(2,1)S(1)} %collective-permute-done.10.refs_1_, s32[1,256]{1,0:T(1,128)S(1)} %bitcast.115, bf16[2048,4096]{1,0:T(8,128)(2,1)S(1)} %bitcast.101), custom_call_target="tpu_custom_call" | custom-call | tf_op jit(solution)/shard_map/pallas_call | solution.py:62
  144.6 6.9 %collective-permute-start.15 = (bf16[128,512]{1,0:T(8,128)(2,1)S(1)}, bf16[128,512]{1,0:T(8,128)(2,1)S(1)}, u32[]{:S(2)}, u32[]{:S(2)}) collective-permute-start(bf16[128,512]{1,0:T(8,128)(2,1)S(1)} %get-tuple-element.66), channel_id=1, source_target_pairs={{0,4},{2,6},{4,0},{6,2},{8,12},{10,14},{12,8},{14,10},{1,5},{3,7},... | collective-permute-start | bytes 393224 | tf_op jit(solution)/shard_map/ppermute | solution.py:147
  153.3 13.2 %collective-permute-done.13.refs_1_ = bf16[128,4096]{1,0:T(8,128)(2,1)S(1)} collective-permute-done((bf16[128,4096]{1,0:T(8,128)(2,1)S(1)}, bf16[128,4096]{1,0:T(8,128)(2,1)S(1)}, u32[]{:S(2)}, u32[]{:S(2)}) %collective-permute-start.13) | collective-permute-done | bytes 1048608 | tf_op jit(solution)/shard_map/ppermute | solution.py:153
  167.4 5.4 %shard_map.72 = f32[64,256]{1,0:T(8,128)S(1)} custom-call(s32[1]{0:T(128)} %bitcast.66.held_ref, bf16[128,4096]{1,0:T(8,128)(2,1)S(1)} %collective-permute-done.12.refs_0_, bf16[128,4096]{1,0:T(8,128)(2,1)S(1)} %collective-permute-done.13.refs_1_, s32[1,256]{1,0:T(1,128)S(1)} %bitcast.109, bf16[2048,4096]{1,0:T(8,128)(2,1)S(1)} %bitcast.103), custom_call_target="tpu_custom_call" | custom-call | tf_op jit(solution)/shard_map/pallas_call | solution.py:62
  172.9 3.4 %collective-permute-done.18 = bf16[128,512]{1,0:T(8,128)(2,1)S(1)} collective-permute-done((bf16[128,512]{1,0:T(8,128)(2,1)S(1)}, bf16[128,512]{1,0:T(8,128)(2,1)S(1)}, u32[]{:S(2)}, u32[]{:S(2)}) %collective-permute-start.18) | collective-permute-done | bytes 131104 | tf_op jit(solution)/shard_map/ppermute | solution.py:147
  178.3 2.1 %collective-permute-start.21 = (bf16[128,512]{1,0:T(8,128)(2,1)S(1)}, bf16[128,512]{1,0:T(8,128)(2,1)S(1)}, u32[]{:S(2)}, u32[]{:S(2)}) collective-permute-start(bf16[128,512]{1,0:T(8,128)(2,1)S(1)} %get-tuple-element.62), channel_id=1, source_target_pairs={{0,14},{2,12},{4,10},{6,8},{8,6},{10,4},{12,2},{14,0},{1,15},{3,13... | collective-permute-start | bytes 393224 | tf_op jit(solution)/shard_map/ppermute | solution.py:147
  183.8 3.7 %collective-permute-done.21 = bf16[128,512]{1,0:T(8,128)(2,1)S(1)} collective-permute-done((bf16[128,512]{1,0:T(8,128)(2,1)S(1)}, bf16[128,512]{1,0:T(8,128)(2,1)S(1)}, u32[]{:S(2)}, u32[]{:S(2)}) %collective-permute-start.21) | collective-permute-done | bytes 131104 | tf_op jit(solution)/shard_map/ppermute | solution.py:147
  (140 shorter events, 40.0 us)
Async XLA Ops:
  6.5 175.8 %reduce-scatter.2.cloned.1.call-start = ((), (), s32[]{:S(2)}) async-start(), calls=%async_computation.2 | async-start | bytes 1572864 | tf_op jit(solution)/shard_map/reduce_scatter | solution.py:190
  6.5 49.1 %collective-permute-start.1 = (bf16[256,4096]{1,0:T(8,128)(2,1)}, bf16[256,4096]{1,0:T(8,128)(2,1)}, u32[]{:S(2)}, u32[]{:S(2)}) collective-permute-start(bf16[256,4096]{1,0:T(8,128)(2,1)} %rows_ref.1), channel_id=1, source_target_pairs={{0,4},{2,6},{4,0},{6,2},{8,12},{10,14},{12,8},{14,10},{1,5},{3,7},... | collective-permute-start | bytes 6291464 | tf_op jit(solution)/shard_map/ppermute | solution.py:147
  9.6 46.0 %collective-permute-start.2 = (bf16[256,4096]{1,0:T(8,128)(2,1)}, bf16[256,4096]{1,0:T(8,128)(2,1)}, u32[]{:S(2)}, u32[]{:S(2)}) collective-permute-start(bf16[256,4096]{1,0:T(8,128)(2,1)} %rows_ref.1), channel_id=1, source_target_pairs={{4,8},{6,10},{8,4},{10,6},{5,9},{7,11},{9,5},{11,7},{20,24},{22,26... | collective-permute-start | bytes 6291464 | tf_op jit(solution)/shard_map/ppermute | solution.py:150
  16.5 25.0 %collective-permute-start = (bf16[128,4096]{1,0:T(8,128)(2,1)}, bf16[128,4096]{1,0:T(8,128)(2,1)}, u32[]{:S(2)}, u32[]{:S(2)}) collective-permute-start(bf16[128,4096]{1,0:T(8,128)(2,1)} %convolution_convert_fusion.9), channel_id=1, source_target_pairs={{0,2},{2,0},{4,6},{6,4},{8,10},{10,8},{12,14},{14,12},{1,3},{3,1},... | collective-permute-start | bytes 3145736 | tf_op jit(solution)/shard_map/ppermute | solution.py:147
  27.6 33.1 %all-to-all-start = ((s32[8,1,256]{2,1,0:T(1,128)}), s32[8,1,256]{2,1,0:T(1,128)S(1)}, u32[]{:S(2)}, u32[]{:S(2)}) async-start(s32[8,1,256]{2,1,0:T(1,128)} %broadcast_in_dim.152), calls=%async_computation.1 | async-start | bytes 16384 | tf_op jit(solution)/shard_map/all_to_all | solution.py:187
  55.6 5.1 %collective-permute-start.3 = (s32[1,256]{1,0:T(1,128)S(1)}, s32[1,256]{1,0:T(1,128)S(1)}, u32[]{:S(2)}, u32[]{:S(2)}) collective-permute-start(s32[1,256]{1,0:T(1,128)S(1)} %bitcast.142), channel_id=1, source_target_pairs={{0,1},{1,0},{2,3},{3,2},{4,5},{5,4},{6,7},{7,6},{8,9},{9,8},{10,11... | collective-permute-start | bytes 3080 | tf_op jit(solution)/shard_map/ppermute | solution.py:93
  55.6 52.7 %collective-permute-start.8 = (bf16[256,4096]{1,0:T(8,128)(2,1)}, bf16[256,4096]{1,0:T(8,128)(2,1)}, u32[]{:S(2)}, u32[]{:S(2)}) collective-permute-start(bf16[256,4096]{1,0:T(8,128)(2,1)} %collective-permute-done.2), channel_id=1, source_target_pairs={{4,0},{6,2},{8,12},{10,14},{5,1},{7,3},{9,13},{11,15},{20,16},{22,... | collective-permute-start | bytes 6291464 | tf_op jit(solution)/shard_map/ppermute | solution.py:153
  56.9 38.4 %collective-permute-start.7 = (bf16[256,4096]{1,0:T(8,128)(2,1)}, bf16[256,4096]{1,0:T(8,128)(2,1)S(1)}, u32[]{:S(2)}, u32[]{:S(2)}) collective-permute-start(bf16[256,4096]{1,0:T(8,128)(2,1)} %collective-permute-done.1), channel_id=1, source_target_pairs={{4,8},{6,10},{8,4},{10,6},{5,9},{7,11},{9,5},{11,7},{20,24},{22,26... | collective-permute-start | bytes 6291464 | tf_op jit(solution)/shard_map/ppermute | solution.py:150
  66.0 23.9 %collective-permute-start.6 = (bf16[128,4096]{1,0:T(8,128)(2,1)}, bf16[128,4096]{1,0:T(8,128)(2,1)S(1)}, u32[]{:S(2)}, u32[]{:S(2)}) collective-permute-start(bf16[128,4096]{1,0:T(8,128)(2,1)} %convolution_convert_fusion.7), channel_id=1, source_target_pairs={{0,2},{2,0},{4,6},{6,4},{8,10},{10,8},{12,14},{14,12},{1,3},{3,1},... | collective-permute-start | bytes 3145736 | tf_op jit(solution)/shard_map/ppermute | solution.py:147
  71.7 79.9 %collective-permute-start.5 = (bf16[128,4096]{1,0:T(8,128)(2,1)}, bf16[128,4096]{1,0:T(8,128)(2,1)S(1)}, u32[]{:S(2)}, u32[]{:S(2)}) collective-permute-start(bf16[128,4096]{1,0:T(8,128)(2,1)} %convolution_convert_fusion.5), channel_id=1, source_target_pairs={{4,6},{6,4},{8,10},{10,8},{5,7},{7,5},{9,11},{11,9},{20,22},{22,20... | collective-permute-start | bytes 3145736 | tf_op jit(solution)/shard_map/ppermute | solution.py:176
  87.3 1.3 collective-permute-start.4
  110.5 25.1 %collective-permute-start.10 = (bf16[128,4096]{1,0:T(8,128)(2,1)S(1)}, bf16[128,4096]{1,0:T(8,128)(2,1)S(1)}, u32[]{:S(2)}, u32[]{:S(2)}) collective-permute-start(bf16[128,4096]{1,0:T(8,128)(2,1)S(1)} %convolution_convert_fusion.2), channel_id=1, source_target_pairs={{0,2},{2,0},{4,6},{6,4},{8,10},{10,8},{12,14},{14,12},{1,3},{3,1},... | collective-permute-start | bytes 3145736 | tf_op jit(solution)/shard_map/ppermute | solution.py:147
  112.1 1.4 collective-permute-start.9
  112.2 39.5 %collective-permute-start.12 = (bf16[128,4096]{1,0:T(8,128)(2,1)S(1)}, bf16[128,4096]{1,0:T(8,128)(2,1)S(1)}, u32[]{:S(2)}, u32[]{:S(2)}) collective-permute-start(bf16[128,4096]{1,0:T(8,128)(2,1)S(1)} %convolution_convert_fusion.3), channel_id=1, source_target_pairs={{4,0},{6,2},{8,12},{10,14},{5,1},{7,3},{9,13},{11,15},{20,16},{22,... | collective-permute-start | bytes 3145736 | tf_op jit(solution)/shard_map/ppermute | solution.py:153
  114.7 51.8 %collective-permute-start.13 = (bf16[128,4096]{1,0:T(8,128)(2,1)S(1)}, bf16[128,4096]{1,0:T(8,128)(2,1)S(1)}, u32[]{:S(2)}, u32[]{:S(2)}) collective-permute-start(bf16[128,4096]{1,0:T(8,128)(2,1)S(1)} %convolution_convert_fusion.1), channel_id=1, source_target_pairs={{4,2},{6,0},{8,14},{10,12},{5,3},{7,1},{9,15},{11,13},{20,18},{22,... | collective-permute-start | bytes 3145736 | tf_op jit(solution)/shard_map/ppermute | solution.py:153
  140.9 1.3 collective-permute-start.11
  143.0 29.8 %collective-permute-start.14 = (bf16[128,512]{1,0:T(8,128)(2,1)S(1)}, bf16[128,512]{1,0:T(8,128)(2,1)S(1)}, u32[]{:S(2)}, u32[]{:S(2)}) collective-permute-start(bf16[128,512]{1,0:T(8,128)(2,1)S(1)} %slice.195), channel_id=1, source_target_pairs={{0,2},{2,0},{4,6},{6,4},{8,10},{10,8},{12,14},{14,12},{1,3},{3,1},... | collective-permute-start | bytes 393224 | tf_op jit(solution)/shard_map/ppermute | solution.py:147
  144.6 28.2 %collective-permute-start.15 = (bf16[128,512]{1,0:T(8,128)(2,1)S(1)}, bf16[128,512]{1,0:T(8,128)(2,1)S(1)}, u32[]{:S(2)}, u32[]{:S(2)}) collective-permute-start(bf16[128,512]{1,0:T(8,128)(2,1)S(1)} %get-tuple-element.66), channel_id=1, source_target_pairs={{0,4},{2,6},{4,0},{6,2},{8,12},{10,14},{12,8},{14,10},{1,5},{3,7},... | collective-permute-start | bytes 393224 | tf_op jit(solution)/shard_map/ppermute | solution.py:147
  151.6 21.3 %collective-permute-start.16 = (bf16[128,512]{1,0:T(8,128)(2,1)S(1)}, bf16[128,512]{1,0:T(8,128)(2,1)S(1)}, u32[]{:S(2)}, u32[]{:S(2)}) collective-permute-start(bf16[128,512]{1,0:T(8,128)(2,1)S(1)} %get-tuple-element.65), channel_id=1, source_target_pairs={{0,6},{2,4},{4,2},{6,0},{8,14},{10,12},{12,10},{14,8},{1,7},{3,5},... | collective-permute-start | bytes 393224 | tf_op jit(solution)/shard_map/ppermute | solution.py:147
  151.7 21.2 %collective-permute-start.17 = (bf16[128,512]{1,0:T(8,128)(2,1)S(1)}, bf16[128,512]{1,0:T(8,128)(2,1)S(1)}, u32[]{:S(2)}, u32[]{:S(2)}) collective-permute-start(bf16[128,512]{1,0:T(8,128)(2,1)S(1)} %get-tuple-element.64), channel_id=1, source_target_pairs={{0,8},{2,10},{4,12},{6,14},{8,0},{10,2},{12,4},{14,6},{1,9},{3,11}... | collective-permute-start | bytes 393224 | tf_op jit(solution)/shard_map/ppermute | solution.py:147
  166.5 9.8 %collective-permute-start.18 = (bf16[128,512]{1,0:T(8,128)(2,1)S(1)}, bf16[128,512]{1,0:T(8,128)(2,1)S(1)}, u32[]{:S(2)}, u32[]{:S(2)}) collective-permute-start(bf16[128,512]{1,0:T(8,128)(2,1)S(1)} %get-tuple-element.63), channel_id=1, source_target_pairs={{0,10},{2,8},{4,14},{6,12},{8,2},{10,0},{12,6},{14,4},{1,11},{3,9}... | collective-permute-start | bytes 393224 | tf_op jit(solution)/shard_map/ppermute | solution.py:147
  176.3 1.3 collective-permute-start.19
  178.3 9.2 %collective-permute-start.21 = (bf16[128,512]{1,0:T(8,128)(2,1)S(1)}, bf16[128,512]{1,0:T(8,128)(2,1)S(1)}, u32[]{:S(2)}, u32[]{:S(2)}) collective-permute-start(bf16[128,512]{1,0:T(8,128)(2,1)S(1)} %get-tuple-element.62), channel_id=1, source_target_pairs={{0,14},{2,12},{4,10},{6,8},{8,6},{10,4},{12,2},{14,0},{1,15},{3,13... | collective-permute-start | bytes 393224 | tf_op jit(solution)/shard_map/ppermute | solution.py:147
  180.4 8.2 %collective-permute-start.20 = (bf16[128,512]{1,0:T(8,128)(2,1)S(1)}, bf16[128,512]{1,0:T(8,128)(2,1)S(1)}, u32[]{:S(2)}, u32[]{:S(2)}) collective-permute-start(bf16[128,512]{1,0:T(8,128)(2,1)S(1)} %get-tuple-element.61), channel_id=1, source_target_pairs={{0,12},{2,14},{4,8},{6,10},{8,4},{10,6},{12,0},{14,2},{1,13},{3,15... | collective-permute-start | bytes 393224 | tf_op jit(solution)/shard_map/ppermute | solution.py:147
  (10 other events, 175.9 us)
Sparse Core Ops, SparseCore 0:
  27.1 8.3 reduce-scatter.1
